TPU v7x, 256 devices: a whole 4x4x8 slice. The times are simulated.
256 devices in a mesh: log: 64 (over y, z, core), pix: 4 (over x).
Axes of the slice: x: 4, y: 4, z: 8, core: 2. Of those that a mesh axis runs over, the one named last changes fastest.
Arguments:
- features: bfloat16 [1024, 1536, 128], P('log', 'pix'), may hold values from -4.5 to 4.5
- endpoint_owner: int32 [1792, 1], P('log'), may hold values from 0 to 63; in each aligned block of 28 rows (0 to 27, 28 to 55, ...) no two rows name the same one
- endpoint_frame: int32 [1792, 1], P('log'), may hold values from 0 to 15
- grad_matched: bfloat16 [896, 1536, 128], P('log', 'pix'), may hold values from -6 to 6
Outputs:
- grad_features: float32 [1024, 1536, 128], P('log', 'pix')
Inputs may be any that keep to these rules, and one draw needn't show every extreme that they name: `endpoint_owner`: within the (28) rows of one device no owner is named more than 1 times, a bound that some block reaches.
All inputs are finite; a program needn't handle non-finite values.
Results may differ from a plain program's by a relative error of at most 0.0075.
Values may be sent and summed in bfloat16 or wider, within the bound.
No kernel may reach another device: no remote copies, remote signals or barrier semaphores. Data moves between devices by JAX's collectives and lax.ppermute only.
A program may use at most 128 MiB of HBM per device.

v0:
```python
import jax
import jax.numpy as jnp
from jax import lax
from jax.sharding import PartitionSpec as P


def softmax_parts(query, keys, scale):
    scores = jnp.dot(query, keys.T, preferred_element_type=jnp.float32) * scale
    top = jnp.max(scores, axis=1, keepdims=True)
    expo = jnp.exp(scores - top)
    total = jnp.sum(expo, axis=1, keepdims=True)
    return (top, total, expo / total)


def edge_terms(query, key_all, cotangent, scale):
    top, total, probs = softmax_parts(query, key_all, scale)
    probs_low = probs.astype(jnp.bfloat16)
    matched = jnp.dot(probs_low, key_all, preferred_element_type=jnp.float32)
    delta = jnp.sum(cotangent.astype(jnp.float32) * matched, axis=1, keepdims=True)
    dprobs = jnp.dot(cotangent, key_all.T, preferred_element_type=jnp.float32)
    dscores = (probs * (dprobs - delta)).astype(jnp.bfloat16)
    grad_query = jnp.dot(dscores, key_all, preferred_element_type=jnp.float32) * scale
    grad_keys = jnp.dot(dscores.T, query, preferred_element_type=jnp.float32) * scale
    grad_keys = grad_keys + jnp.dot(probs_low.T, cotangent, preferred_element_type=jnp.float32)
    return (grad_query, grad_keys)


def shards(features, endpoint_owner, endpoint_frame, grad_matched):
    peers = lax.axis_size("log")
    frames_dev, rows, chans = features.shape
    ends = endpoint_owner.shape[0]
    slots_each = (ends + peers - 1) // peers
    slot_total = peers * slots_each
    scale = chans ** (-0.5)
    owner = endpoint_owner[:, 0]
    local = endpoint_frame[:, 0]
    order = jnp.arange(ends)
    same = owner[:, None] == owner[None, :]
    earlier = order[None, :] < order[:, None]
    rank = jnp.sum((same & earlier).astype(jnp.int32), axis=1)
    slot = owner * slots_each + rank
    picks = slot[None, :] == jnp.arange(slot_total)[:, None]
    request = jnp.sum(jnp.where(picks, local[None, :], 0), axis=1)
    request = request.reshape(peers, slots_each)
    wanted = lax.all_to_all(request, "log", split_axis=0, concat_axis=0, tiled=True)
    served = jnp.take(features, wanted, axis=0)
    answer = lax.all_to_all(served, "log", split_axis=0, concat_axis=0, tiled=True)
    fetched = answer
    fetched = fetched.reshape(slot_total, rows, chans)
    queries = jnp.take(fetched, slot[0::2], axis=0)
    own_keys = jnp.take(fetched, slot[1::2], axis=0)
    keys = lax.all_gather(own_keys, "pix", axis=1, tiled=True)

    def edge_local(args):
        return edge_terms(args[0], args[1], args[2], scale)

    grad_query, partial_keys = lax.map(edge_local, (queries, keys, grad_matched))
    grad_target = lax.psum_scatter(
        partial_keys.astype(jnp.bfloat16), "pix", scatter_dimension=1, tiled=True
    )
    stacked = jnp.stack([grad_query.astype(jnp.bfloat16), grad_target], axis=1)
    stacked = stacked.reshape(ends, rows * chans)
    placing = picks.astype(jnp.bfloat16)
    outgoing = jnp.dot(placing, stacked, preferred_element_type=jnp.float32).astype(jnp.bfloat16)
    outgoing = outgoing.reshape(peers, slots_each, rows, chans)
    incoming = lax.all_to_all(outgoing, "log", split_axis=0, concat_axis=0, tiled=True)
    incoming = incoming.reshape(slot_total, rows * chans)
    landing = (wanted.reshape(slot_total)[None, :] == jnp.arange(frames_dev)[:, None]).astype(
        jnp.bfloat16
    )
    grads = jnp.dot(landing, incoming, preferred_element_type=jnp.float32)
    return grads.reshape(frames_dev, rows, chans)


def solution(mesh):
    in_specs = (P("log", "pix", None), P("log", None), P("log", None), P("log", "pix", None))
    out_specs = P("log", "pix", None)
    return jax.shard_map(shards, mesh=mesh, in_specs=in_specs, out_specs=out_specs, check_vma=False)
```

profile of v0, /device:TPU:1, one launch (start us, length us, event | category | flops | bytes accessed | tf_op | source)
XLA Modules:
  0.0 655.3 jit_solution(7332500759947476944)
XLA Ops:
  9.0 22.2 %all_to_all.19 = s32[64,1,1]{2,1,0:T(1,128)S(1)} all-to-all(s32[64,1,1]{2,1,0:T(1,128)S(1)} %copy.23), channel_id=1, replica_groups=mesh['log'=64,'pix'=4] {'log'}, dimensions={0} | all-to-all | bytes 512 | tf_op jit(solution)/shard_map/all_to_all | solution.py:45
  33.7 4.0 gather_fusion
  37.7 6.1 bitcast_select_fusion
  43.8 5.7 all-to-all-start.1
  49.8 140.7 %all-to-all-done.1 = bf16[64,1,384,128]{3,2,1,0:T(8,128)(2,1)} async-done(((bf16[64,1,384,128]{3,2,1,0:T(8,128)(2,1)}), bf16[64,1,384,128]{3,2,1,0:T(8,128)(2,1)}, u32[]{:S(2)}, u32[]{:S(2)}) %all-to-all-start.1) | async-done | bytes 6291488 | tf_op jit(solution)/shard_map/all_to_all | solution.py:47
  190.5 3.6 gather_fusion.2
  195.8 3.6 gather_fusion.1
  199.6 54.2 %all-gather.2.cloned.1.call-done = bf16[14,1536,128]{2,1,0:T(8,128)(2,1)} async-done(((bf16[14,384,128]{2,1,0:T(8,128)(2,1)}), bf16[14,1536,128]{2,1,0:T(8,128)(2,1)}) %all-gather.2.cloned.1.call-update) | async-done | bytes 5505040 | tf_op jit(solution)/shard_map/all_gather | solution.py:52
  253.7 162.7 %while.12 = (s32[]{:T(128)}, bf16[14,384,128]{2,1,0:T(8,128)(2,1)}, bf16[14,1536,128]{2,1,0:T(8,128)(2,1)}, bf16[14,384,128]{2,1,0:T(8,128)(2,1)S(1)}, bf16[14,1...) while((s32[]{:T(128)}, bf16[14,384,128]{2,1,0:T(8,128)(2,1)}, ...), condition=%wide.region_6.8_spmd, body=%wide.region_2.7_spmd.sunk | while | flops 915405696 | bytes 20370016 | solution.py:57
  256.8 1.7 fusion.73
  258.5 1.7 fusion.74
  260.8 2.1 fusion.75
  262.9 2.4 fusion.76
  270.1 1.7 fusion.74
  272.4 2.1 fusion.75
  274.5 2.5 fusion.76
  280.0 1.7 fusion.73
  281.8 1.7 fusion.74
  284.0 2.1 fusion.75
  286.1 2.5 fusion.76
  293.4 1.7 fusion.74
  295.7 2.1 fusion.75
  297.8 2.5 fusion.76
  305.0 1.7 fusion.74
  307.3 2.1 fusion.75
  309.4 2.5 fusion.76
  314.9 1.7 fusion.73
  316.7 1.7 fusion.74
  318.9 2.1 fusion.75
  321.1 2.4 fusion.76
  328.3 1.7 fusion.74
  330.5 2.1 fusion.75
  332.7 2.4 fusion.76
  338.2 1.7 fusion.73
  339.9 1.7 fusion.74
  342.2 2.1 fusion.75
  344.3 2.5 fusion.76
  351.5 1.7 fusion.74
  353.8 2.1 fusion.75
  355.9 2.4 fusion.76
  363.1 1.7 fusion.74
  365.4 2.1 fusion.75
  367.5 2.5 fusion.76
  374.7 1.7 fusion.74
  377.0 2.1 fusion.75
  379.1 2.5 fusion.76
  384.6 1.7 fusion.73
  386.3 1.7 fusion.74
  388.6 2.1 fusion.75
  390.7 2.5 fusion.76
  398.0 1.7 fusion.74
  400.2 2.1 fusion.75
  402.3 2.5 fusion.76
  409.6 1.7 fusion.74
  411.9 2.1 fusion.75
  414.0 2.4 fusion.76
  416.4 60.9 %reduce-scatter.2.cloned.1.call-done = bf16[14,384,128]{2,1,0:T(8,128)(2,1)} async-done(((bf16[14,1536,128]{2,1,0:T(8,128)(2,1)}), bf16[14,384,128]{2,1,0:T(8,128)(2,1)}) %reduce-scatter.2.cloned.1.call-update) | async-done | bytes 1376272 | tf_op jit(solution)/shard_map/reduce_scatter | solution.py:58
  479.4 2.0 copy.31
  481.5 1.9 fusion.35
  483.4 4.4 copy.32
  487.8 10.8 %all-to-all-start.2 = ((bf16[64,1,384,128]{3,2,1,0:T(8,128)(2,1)}), bf16[64,1,384,128]{3,2,1,0:T(8,128)(2,1)}, u32[]{:S(2)}, u32[]{:S(2)}) async-start(bf16[64,1,384,128]{3,2,1,0:T(8,128)(2,1)} %bitcast.102), calls=%async_computation.3 | async-start | bytes 12582912 | tf_op jit(solution)/shard_map/all_to_all | solution.py:66
  499.8 139.6 %all-to-all-done.2 = bf16[64,1,384,128]{3,2,1,0:T(8,128)(2,1)} async-done(((bf16[64,1,384,128]{3,2,1,0:T(8,128)(2,1)}), bf16[64,1,384,128]{3,2,1,0:T(8,128)(2,1)}, u32[]{:S(2)}, u32[]{:S(2)}) %all-to-all-start.2) | async-done | bytes 6291488 | tf_op jit(solution)/shard_map/all_to_all | solution.py:66
  639.4 6.4 fusion.32
  645.8 2.6 copy.28
  (112 shorter events, 75.6 us)
Async XLA Ops:
  6.5 27.2 %copy-start = (bf16[16,384,128]{2,1,0:T(8,128)(2,1)S(1)}, bf16[16,384,128]{2,1,0:T(8,128)(2,1)}, u32[]{:S(2)}) copy-start(bf16[16,384,128]{2,1,0:T(8,128)(2,1)} %param.8) | copy-start | bytes 4718596
  43.8 146.6 %all-to-all-start.1 = ((bf16[64,1,384,128]{3,2,1,0:T(8,128)(2,1)}), bf16[64,1,384,128]{3,2,1,0:T(8,128)(2,1)}, u32[]{:S(2)}, u32[]{:S(2)}) async-start(bf16[64,1,384,128]{3,2,1,0:T(8,128)(2,1)} %bitcast_select_fusion), calls=%async_computation.1 | async-start | bytes 12582912 | tf_op jit(solution)/shard_map/all_to_all | solution.py:47
  49.6 204.2 %all-gather.2.cloned.1.call-start = ((), (), s32[]{:S(2)}) async-start(), calls=%async_computation.4 | async-start | bytes 6881280 | tf_op jit(solution)/shard_map/all_gather | solution.py:52
  195.4 281.9 %reduce-scatter.2.cloned.1.call-start = ((), (), s32[]{:S(2)}) async-start(), calls=%async_computation.5 | async-start | bytes 6881280 | tf_op jit(solution)/shard_map/reduce_scatter | solution.py:58
  416.4 60.9 %copy-start.2 = (bf16[14,384,128]{2,1,0:T(8,128)(2,1)S(1)}, bf16[14,384,128]{2,1,0:T(8,128)(2,1)}, u32[]{:S(2)}) copy-start(bf16[14,384,128]{2,1,0:T(8,128)(2,1)} %get-tuple-element.39) | copy-start | bytes 4128772
  487.8 151.7 %all-to-all-start.2 = ((bf16[64,1,384,128]{3,2,1,0:T(8,128)(2,1)}), bf16[64,1,384,128]{3,2,1,0:T(8,128)(2,1)}, u32[]{:S(2)}, u32[]{:S(2)}) async-start(bf16[64,1,384,128]{3,2,1,0:T(8,128)(2,1)} %bitcast.102), calls=%async_computation.3 | async-start | bytes 12582912 | tf_op jit(solution)/shard_map/all_to_all | solution.py:66
  639.4 9.0 %copy-start.1 = (bf16[16,384,128]{2,1,0:T(8,128)(2,1)S(1)}, bf16[16,384,128]{2,1,0:T(8,128)(2,1)}, u32[]{:S(2)}) copy-start(bf16[16,384,128]{2,1,0:T(8,128)(2,1)} %param.8) | copy-start | bytes 4718596
Sparse Core Ops, SparseCore 0:
  195.5 58.1 all-gather.1
  416.6 60.6 reduce-scatter.1
where the time goes:
time: 659 us; the launch traced here: 655 us
  waiting for transfers between devices  395 us (60%)
  matrix products  150 us (23%)
  local copies, waits for them, and re-layouts  35.4 us (5%)
  blocking collectives  22.2 us (3%)
  other arithmetic  21.9 us (3%)
  starting transfers between devices  16.8 us (3%)
  between operations  13.6 us (2%)
    all_to_all x1, waiting for transfers between devices, shards(): lax.all_to_all(served, 'log', split_axis=0, concat_axis=0, tiled=True)  141 us
    all_to_all x1, waiting for transfers between devices, shards(): lax.all_to_all(outgoing, 'log', split_axis=0, concat_axis=0, tiled=True)  140 us
    reduce_scatter x1, waiting for transfers between devices, shards(): lax.psum_scatter(partial_keys.astype(jnp.bfloat16), 'pix', scatter_dimens...  60.9 us
    all_gather x1, waiting for transfers between devices, shards(): keys = lax.all_gather(own_keys, 'pix', axis=1, tiled=True)  54.2 us
    dot_general x14, matrix products, edge_terms(): jnp.dot(probs_low.T, cotangent, preferred_element_type=jnp.float32)  34.4 us
    dot_general x14, matrix products, edge_terms(): jnp.dot(dscores, key_all, preferred_element_type=jnp.float32) * scale  29.6 us
    dot_general x14, matrix products, edge_terms(): dprobs = jnp.dot(cotangent, key_all.T, preferred_element_type=jnp.float32)  24.4 us
    dot_general x14, matrix products, edge_terms(): matched = jnp.dot(probs_low, key_all, preferred_element_type=jnp.float32)  24.1 us
  transfers between devices with their start and end apart: 4, of which 4 were waited for; matrix products, arithmetic and copies ran while one was open for 1% of the time, Pallas kernels for 0%

commit v1 on v0

v1 whole, which is shorter than its diff:
```python
import functools
import math

import jax
import jax.numpy as jnp
from jax import lax
from jax.experimental import pallas as pl
from jax.experimental.pallas import tpu as pltpu
from jax.sharding import PartitionSpec as P

F32 = jnp.float32
BF16 = jnp.bfloat16
LANES = 128
PAD_ID = 2047
VMEM_LIMIT = 48 * 2**20


def dot(a, b, ca, cb):
    return lax.dot_general(a, b, (((ca,), (cb,)), ((), ())), preferred_element_type=F32)


def spread_kernel(peers, piece, feat_ref, out_ref, wide):
    frames, rows, chans = feat_ref.shape
    for f in range(frames):
        wide[f * rows : (f + 1) * rows, :] = feat_ref[f].astype(F32)

    def one(d, carry):
        for k in range(piece):
            block = wide[pl.ds(k * peers + d, frames, stride=rows), :]
            out_ref[d, k * frames : (k + 1) * frames, :] = block.astype(BF16)
        return carry

    lax.fori_loop(0, peers, one, 0)


def spread(features, peers):
    frames, rows, chans = features.shape
    piece = rows // peers
    return pl.pallas_call(
        functools.partial(spread_kernel, peers, piece),
        out_shape=jax.ShapeDtypeStruct((peers, piece * frames, chans), BF16),
        in_specs=[pl.BlockSpec(memory_space=pltpu.VMEM)],
        out_specs=pl.BlockSpec(memory_space=pltpu.VMEM),
        scratch_shapes=[pltpu.VMEM((frames * rows, chans), F32)],
        compiler_params=pltpu.CompilerParams(vmem_limit_bytes=VMEM_LIMIT),
        name="spread",
    )(features)


def split_ids(ids_ref):
    ids = ids_ref[...]
    high = lax.shift_right_logical(ids, 4)
    low = ids - high * 16
    return high.astype(F32).astype(BF16), low.astype(F32).astype(BF16)


def id_column(ids_ref, part, slots):
    peers = ids_ref.shape[0]
    count = peers * slots
    high, low = split_ids(ids_ref)
    row = lax.broadcasted_iota(jnp.int32, (count, peers), 0)
    col = lax.broadcasted_iota(jnp.int32, (count, peers), 1)
    pick = (lax.div(row, slots) == col).astype(F32).astype(BF16)
    every = dot(pick, high, 1, 0) * 16.0 + dot(pick, low, 1, 0)
    row = lax.broadcasted_iota(jnp.int32, (count, LANES), 0)
    lane = lax.broadcasted_iota(jnp.int32, (count, LANES), 1)
    mine = lane == part * slots + lax.rem(row, slots)
    return jnp.sum(jnp.where(mine, every, 0.0), axis=1, keepdims=True)


def id_row(ids_ref, part, slots):
    peers = ids_ref.shape[0]
    count = peers * slots
    high, low = split_ids(ids_ref)
    row = lax.broadcasted_iota(jnp.int32, (LANES, count), 0)
    col = lax.broadcasted_iota(jnp.int32, (LANES, count), 1)
    pick = (row == part * slots + lax.rem(col, slots)).astype(F32).astype(BF16)
    every = dot(high, pick, 1, 0) * 16.0 + dot(low, pick, 1, 0)
    row = lax.broadcasted_iota(jnp.int32, (peers, count), 0)
    col = lax.broadcasted_iota(jnp.int32, (peers, count), 1)
    return jnp.sum(jnp.where(lax.div(col, slots) == row, every, 0.0), axis=0, keepdims=True)


def fetch_kernel(slots, piece, frames, held_ref, ids_ref, out_ref, table):
    part = pl.program_id(0)
    peers = held_ref.shape[0]
    total = peers * frames

    @pl.when(part == 0)
    def _():
        for k in range(piece):
            block = held_ref[:, k * frames : (k + 1) * frames, :]
            table[:, k * LANES : (k + 1) * LANES] = block.reshape(total, LANES)

    column = id_column(ids_ref, part, slots)
    count = peers * slots
    lane = lax.broadcasted_iota(jnp.int32, (count, total), 1).astype(F32)
    chosen = jnp.where(column == lane, 1.0, 0.0).astype(BF16)
    rows = dot(chosen, table[...], 1, 0)
    for pair in range(piece // 2):
        halves = [
            rows[:, (2 * pair + h) * LANES : (2 * pair + h + 1) * LANES].reshape(peers, slots, LANES)
            for h in range(2)
        ]
        both = jnp.concatenate(halves, axis=1)
        out_ref[:, pair * 2 * slots : (pair + 1) * 2 * slots, :] = both.astype(BF16)


def fetch(held, ids, parts, slots, piece, frames):
    peers = held.shape[0]
    return pl.pallas_call(
        functools.partial(fetch_kernel, slots, piece, frames),
        grid=(parts,),
        out_shape=jax.ShapeDtypeStruct((parts * peers, piece * slots, LANES), BF16),
        in_specs=[
            pl.BlockSpec(held.shape, lambda p: (0, 0, 0)),
            pl.BlockSpec(ids.shape, lambda p: (0, 0)),
        ],
        out_specs=pl.BlockSpec((peers, piece * slots, LANES), lambda p: (p, 0, 0)),
        scratch_shapes=[pltpu.VMEM((peers * frames, piece * LANES), BF16)],
        compiler_params=pltpu.CompilerParams(vmem_limit_bytes=VMEM_LIMIT),
        name="fetch",
    )(held, ids)


def edge_kernel(
    slots, piece, peers, parts, block, place_ref, held_ref, *refs
):
    cot_refs = refs[:parts]
    out_ref, wide, query, keys, cot, grad_a, grad_b = refs[parts:]
    edge = pl.program_id(0)
    each = piece * slots
    rows = piece * peers
    pixels = parts * rows
    scale = LANES ** (-0.5)
    log2e = math.log2(math.e)

    @pl.when(edge == 0)
    def _():
        def widen(p, carry):
            at = pl.multiple_of(p * 8 * each, 8 * each)
            block8 = held_ref[pl.ds(pl.multiple_of(p * 8, 8), 8)]
            wide[pl.ds(at, 8 * each), :] = block8.astype(F32).reshape(8 * each, LANES)
            return carry

        lax.fori_loop(0, parts * peers // 8, widen, 0)

    def spot(part, k, slot):
        return pl.ds(part * peers * each + k * slots + slot, peers, stride=each)

    for part in range(parts):
        for k in range(piece):
            here = pl.ds(part * rows + k * peers, peers)
            query[here, :] = wide[spot(part, k, 2 * edge), :].astype(BF16)
            keys[here, :] = wide[spot(part, k, 2 * edge + 1), :].astype(BF16)
        at = pl.multiple_of(place_ref[part] * rows, rows)
        cot[pl.ds(at, rows), :] = cot_refs[part][0]

    key_all = keys[...]
    for step in range(pixels // block):
        here = pl.ds(step * block, block)
        q = query[here, :]
        g = cot[here, :]
        scores = dot(q, key_all, 1, 1)
        top = jnp.max(scores, axis=1, keepdims=True)
        expo = jnp.exp2((scores - top) * (scale * log2e))
        total = jnp.sum(expo, axis=1, keepdims=True)
        dprobs = dot(g, key_all, 1, 1)
        inverse = 1.0 / total
        delta = jnp.sum(expo * dprobs, axis=1, keepdims=True) * inverse
        probs = expo * inverse
        probs_low = probs.astype(BF16)
        dscores = (probs * (dprobs - delta)).astype(BF16)
        grad_query = dot(dscores, key_all, 1, 0) * scale
        for sub in range(block // peers):
            at = step * (block // peers) + sub
            wide[spot(at // piece, at % piece, 2 * edge), :] = grad_query[
                sub * peers : (sub + 1) * peers, :
            ]
        first = dot(q, dscores, 0, 0)
        second = dot(g, probs_low, 0, 0)
        if step == 0:
            grad_a[...] = first
            grad_b[...] = second
        else:
            grad_a[...] += first
            grad_b[...] += second
    grad_keys = (grad_a[...] * scale + grad_b[...]).T
    for at in range(pixels // peers):
        wide[spot(at // piece, at % piece, 2 * edge + 1), :] = grad_keys[
            at * peers : (at + 1) * peers, :
        ]

    @pl.when(edge == slots // 2 - 1)
    def _():
        def narrow(p, carry):
            at = pl.multiple_of(p * 8 * each, 8 * each)
            block8 = wide[pl.ds(at, 8 * each), :].reshape(8, each, LANES)
            out_ref[pl.ds(pl.multiple_of(p * 8, 8), 8)] = block8.astype(BF16)
            return carry

        lax.fori_loop(0, parts * peers // 8, narrow, 0)


def edges(held, cotangents, places, slots, piece, peers):
    parts = len(cotangents)
    rows = piece * peers
    pixels = parts * rows
    per_edge = pl.BlockSpec((1, rows, LANES), lambda e, place: (e, 0, 0))
    whole = pl.BlockSpec(held.shape, lambda e, place: (0, 0, 0))
    block = 512
    return pl.pallas_call(
        functools.partial(edge_kernel, slots, piece, peers, parts, block),
        grid_spec=pltpu.PrefetchScalarGridSpec(
            num_scalar_prefetch=1,
            grid=(slots // 2,),
            in_specs=[whole] + [per_edge] * parts,
            out_specs=whole,
            scratch_shapes=[
                pltpu.VMEM((held.shape[0] * held.shape[1], LANES), F32),
                pltpu.VMEM((pixels, LANES), BF16),
                pltpu.VMEM((pixels, LANES), BF16),
                pltpu.VMEM((pixels, LANES), BF16),
                pltpu.VMEM((LANES, pixels), F32),
                pltpu.VMEM((LANES, pixels), F32),
            ],
        ),
        out_shape=jax.ShapeDtypeStruct(held.shape, BF16),
        compiler_params=pltpu.CompilerParams(vmem_limit_bytes=VMEM_LIMIT),
        name="edges",
    )(places, held, *cotangents)


def land_kernel(slots, piece, frames, back_ref, ids_ref, out_ref, total):
    part = pl.program_id(0)
    peers = back_ref.shape[0]
    count = peers * slots
    row = id_row(ids_ref, part, slots)
    every = lax.broadcasted_iota(jnp.int32, (peers * frames, count), 0).astype(F32)
    chosen = jnp.where(row == every, 1.0, 0.0).astype(BF16)
    columns = []
    for pair in range(piece // 2):
        both = back_ref[:, pair * 2 * slots : (pair + 1) * 2 * slots, :].astype(F32)
        for h in range(2):
            half = both[:, h * slots : (h + 1) * slots, :].reshape(count, LANES)
            columns.append(half.astype(BF16))
    sums = dot(chosen, jnp.concatenate(columns, axis=1), 1, 0)

    @pl.when(part == 0)
    def _():
        total[...] = sums

    @pl.when(part > 0)
    def _():
        total[...] += sums

    @pl.when(part == pl.num_programs(0) - 1)
    def _():
        for k in range(piece):
            block = total[:, k * LANES : (k + 1) * LANES].reshape(peers, frames, LANES)
            out_ref[:, k * frames : (k + 1) * frames, :] = block.astype(BF16)


def land(back, ids, parts, slots, piece, frames):
    peers = back.shape[0] // parts
    return pl.pallas_call(
        functools.partial(land_kernel, slots, piece, frames),
        grid=(parts,),
        out_shape=jax.ShapeDtypeStruct((peers, piece * frames, LANES), BF16),
        in_specs=[
            pl.BlockSpec((peers, piece * slots, LANES), lambda p: (p, 0, 0)),
            pl.BlockSpec(ids.shape, lambda p: (0, 0)),
        ],
        out_specs=pl.BlockSpec((peers, piece * frames, LANES), lambda p: (0, 0, 0)),
        scratch_shapes=[pltpu.VMEM((peers * frames, piece * LANES), F32)],
        compiler_params=pltpu.CompilerParams(vmem_limit_bytes=VMEM_LIMIT),
        name="land",
    )(back, ids)


def collect_kernel(piece, frames, back_ref, out_ref, wide):
    peers, each, _ = back_ref.shape

    def widen(p, carry):
        at = pl.multiple_of(p * 8 * each, 8 * each)
        block8 = back_ref[pl.ds(pl.multiple_of(p * 8, 8), 8)]
        wide[pl.ds(at, 8 * each), :] = block8.astype(F32).reshape(8 * each, LANES)
        return carry

    lax.fori_loop(0, peers // 8, widen, 0)

    def one(f, carry):
        for k in range(piece):
            block = wide[pl.ds(k * frames + f, peers, stride=each), :]
            out_ref[f, k * peers : (k + 1) * peers, :] = block
        return carry

    lax.fori_loop(0, frames, one, 0)


def collect(back, frames, piece):
    peers, each, _ = back.shape
    return pl.pallas_call(
        functools.partial(collect_kernel, piece, frames),
        out_shape=jax.ShapeDtypeStruct((frames, piece * peers, LANES), F32),
        in_specs=[pl.BlockSpec(memory_space=pltpu.VMEM)],
        out_specs=pl.BlockSpec(memory_space=pltpu.VMEM),
        scratch_shapes=[pltpu.VMEM((peers * each, LANES), F32)],
        compiler_params=pltpu.CompilerParams(vmem_limit_bytes=VMEM_LIMIT),
        name="collect",
    )(back)


def shards(features, endpoint_owner, endpoint_frame, grad_matched):
    peers = lax.axis_size("log")
    parts = lax.axis_size("pix")
    frames, rows, chans = features.shape
    piece = rows // peers
    ends = endpoint_owner.shape[0]
    each = -(-(ends // 2) // parts)
    slots = 2 * each
    me = lax.axis_index("pix")

    ids = (endpoint_owner * frames + endpoint_frame).reshape(1, ends)
    ids = jnp.pad(ids, ((0, 0), (0, LANES - ends)), constant_values=PAD_ID)
    ids = lax.all_gather(ids, "log", axis=0, tiled=True)

    padded = jnp.pad(grad_matched, ((0, parts * each - ends // 2), (0, 0), (0, 0)))
    cotangents = []
    for t in range(parts):
        taker = lax.rem(me + t, parts)
        given = lax.dynamic_slice_in_dim(padded, taker * each, each, axis=0)
        if t:
            given = lax.ppermute(given, "pix", [(p, (p + t) % parts) for p in range(parts)])
        cotangents.append(given)
    places = jnp.stack([lax.rem(me + parts - t, parts) for t in range(parts)])

    held = lax.all_to_all(spread(features, peers), "log", 0, 0, tiled=True)
    sent = fetch(held, ids, parts, slots, piece, frames)
    got = lax.all_to_all(sent, ("pix", "log"), 0, 0, tiled=True)
    grads = edges(got, cotangents, places, slots, piece, peers)
    back = lax.all_to_all(grads, ("pix", "log"), 0, 0, tiled=True)
    sums = land(back, ids, parts, slots, piece, frames)
    mine = lax.all_to_all(sums, "log", 0, 0, tiled=True)
    return collect(mine, frames, piece)


def solution(mesh):
    in_specs = (P("log", "pix", None), P("log", None), P("log", None), P("log", "pix", None))
    out_specs = P("log", "pix", None)
    return jax.shard_map(shards, mesh=mesh, in_specs=in_specs, out_specs=out_specs, check_vma=False)
```

time: 659 us -> 351 us (0.53)
  waiting for transfers between devices: 395 us -> 70.3 us
  blocking collectives: 22.2 us -> 196 us
  matrix products: 150 us -> 0 us
  Pallas kernels: 0 us -> 55.3 us
  local copies, waits for them, and re-layouts: 35.4 us -> 2.56 us
  other arithmetic: 21.9 us -> 0.08 us
  between operations: 13.6 us -> 0.11 us
  starting transfers between devices: 16.8 us -> 27 us
    all_to_all x2, waiting for transfers between devices: 280 us -> 40.5 us  [the longest x1 40.5 us: shards(): got = lax.all_to_all(sent, ('pix', 'log'), 0, 0, tiled=True)]
    dot_general x86 -> x0, matrix products: 150 us -> none  [the longest x14 34.4 us: edge_terms(): jnp.dot(probs_low.T, cotangent, preferred_element_type=jnp.float32)]
    all_to_all x1 -> x2, blocking collectives: 22.2 us -> 125 us  [the longest x1 81.6 us: shards(): back = lax.all_to_all(grads, ('pix', 'log'), 0, 0, tiled=True)]
    all_gather x0 -> x1, blocking collectives: none -> 70.6 us  [shards(): ids = lax.all_gather(ids, 'log', axis=0, tiled=True)]
    reduce_scatter x1 -> x0, waiting for transfers between devices: 60.9 us -> none  [shards(): lax.psum_scatter(partial_keys.astype(jnp.bfloat16), 'pix', scatter_dimens...]
    pallas_call x0 -> x5, Pallas kernels: none -> 55.3 us  [the longest x1 34.5 us: edges(): pl.pallas_call(functools.partial(edge_kernel, slots, piece, peers, parts,...]
    all_gather x1 -> x0, waiting for transfers between devices: 54.2 us -> none  [shards(): keys = lax.all_gather(own_keys, 'pix', axis=1, tiled=True)]
    ppermute x0 -> x3, waiting for transfers between devices: none -> 29.9 us  [shards(): lax.ppermute(given, 'pix', [(p, (p + t) % parts) for p in range(parts)])]
  transfers between devices with their start and end apart: 4 -> 5, of which waited for: 4 -> 3; matrix products, arithmetic and copies ran while one was open for 1% -> 0% of each run, Pallas kernels for 0% -> 0%
where the time goes in v1:
time: 351 us
  blocking collectives  196 us (56%)
  waiting for transfers between devices  70.3 us (20%)
  Pallas kernels  55.3 us (16%)
  starting transfers between devices  27 us (8%)
    all_to_all x1, blocking collectives, shards(): back = lax.all_to_all(grads, ('pix', 'log'), 0, 0, tiled=True)  81.6 us
    all_gather x1, blocking collectives, shards(): ids = lax.all_gather(ids, 'log', axis=0, tiled=True)  70.6 us
    all_to_all x1, blocking collectives, shards(): mine = lax.all_to_all(sums, 'log', 0, 0, tiled=True)  43.4 us
    all_to_all x1, waiting for transfers between devices, shards(): got = lax.all_to_all(sent, ('pix', 'log'), 0, 0, tiled=True)  40.5 us
    pallas_call x1, Pallas kernels, edges(): pl.pallas_call(functools.partial(edge_kernel, slots, piece, peers, parts,...  34.5 us
    ppermute x3, waiting for transfers between devices, shards(): lax.ppermute(given, 'pix', [(p, (p + t) % parts) for p in range(parts)])  29.9 us
    all_to_all x1, starting transfers between devices, shards(): held = lax.all_to_all(spread(features, peers), 'log', 0, 0, tiled=True)  13.3 us
    all_to_all x1, starting transfers between devices, shards(): got = lax.all_to_all(sent, ('pix', 'log'), 0, 0, tiled=True)  8.76 us
  transfers between devices with their start and end apart: 5, of which 3 were waited for; matrix products, arithmetic and copies ran while one was open for 0% of the time, Pallas kernels for 0%

profile of v1, /device:TPU:1, one launch (start us, length us, event | category | flops | bytes accessed | tf_op | source)
XLA Modules:
  0.0 351.1 jit_solution(2995777729681591521)
XLA Ops:
  0.0 0.0 copy-start
  0.0 1.4 copy-done
  1.4 5.0 %spread.1 = bf16[64,96,128]{2,1,0:T(8,128)(2,1)} custom-call(bf16[16,384,128]{2,1,0:T(8,128)(2,1)S(1)} %copy-done), custom_call_target="tpu_custom_call" | custom-call | tf_op jit(solution)/shard_map/spread/pallas_call | solution.py:39
  6.4 0.0 copy-start.2
  6.4 0.0 copy-start.3
  6.4 13.3 %all-to-all-start = ((bf16[64,96,128]{2,1,0:T(8,128)(2,1)}), bf16[64,96,128]{2,1,0:T(8,128)(2,1)S(1)}, u32[]{:S(2)}, u32[]{:S(2)}) async-start(bf16[64,96,128]{2,1,0:T(8,128)(2,1)} %spread.1), calls=%async_computation | async-start | bytes 3145728 | tf_op jit(solution)/shard_map/all_to_all | solution.py:338
  19.7 0.0 copy-done.2
  19.7 0.0 copy-done.3
  19.8 70.6 %all-gather = s32[64,1,128]{2,1,0:T(1,128)S(1)} all-gather(s32[1,1,128]{2,1,0:T(1,128)S(1)} %pad_bitcast_fusion), channel_id=1, replica_groups=mesh['log'=64,'pix'=4] {'log'}, dimensions={0}, use_global_device_ids=true | all-gather | bytes 33280 | tf_op jit(solution)/shard_map/all_gather | solution.py:326
  90.4 0.0 all-to-all-done.held_ref
  90.4 6.0 %fetch.1 = bf16[256,48,128]{2,1,0:T(8,128)(2,1)} custom-call(bf16[64,96,128]{2,1,0:T(8,128)(2,1)S(1)} %all-to-all-done.held_ref, s32[64,128]{1,0:T(8,128)S(1)} %bitcast.9), custom_call_target="tpu_custom_call" | custom-call | tf_op jit(solution)/shard_map/fetch/pallas_call | solution.py:111
  96.4 0.0 copy-start.1
  96.4 8.8 %all-to-all-start.1 = ((bf16[256,48,128]{2,1,0:T(8,128)(2,1)}), bf16[256,48,128]{2,1,0:T(8,128)(2,1)}, u32[]{:S(2)}, u32[]{:S(2)}) async-start(bf16[256,48,128]{2,1,0:T(8,128)(2,1)} %fetch.1), calls=%async_computation.1 | async-start | bytes 6291456 | tf_op jit(solution)/shard_map/all_to_all | solution.py:340
  105.2 0.0 copy-done.1
  105.2 1.1 pad_dynamic-slice_fusion
  106.3 1.4 collective-permute-start
  107.7 2.4 collective-permute-start.1
  110.1 1.2 collective-permute-start.2
  111.3 0.1 pad_add_fusion.place_ref
  111.3 14.1 %collective-permute-done.refs_1_ = bf16[4,384,128]{2,1,0:T(8,128)(2,1)S(1)} collective-permute-done((bf16[4,384,128]{2,1,0:T(8,128)(2,1)}, bf16[4,384,128]{2,1,0:T(8,128)(2,1)S(1)}, u32[]{:S(2)}, u32[]{:S(2)}) %collective-permute-start) | collective-permute-done | bytes 393248 | tf_op jit(solution)/shard_map/ppermute | solution.py:334
  125.4 15.8 %collective-permute-done.1.refs_2_ = bf16[4,384,128]{2,1,0:T(8,128)(2,1)S(1)} collective-permute-done((bf16[4,384,128]{2,1,0:T(8,128)(2,1)}, bf16[4,384,128]{2,1,0:T(8,128)(2,1)S(1)}, u32[]{:S(2)}, u32[]{:S(2)}) %collective-permute-start.1) | collective-permute-done | bytes 393248 | tf_op jit(solution)/shard_map/ppermute | solution.py:334
  141.2 0.0 collective-permute-done.2.refs_3_
  141.2 40.5 %all-to-all-done.1.held_ref = bf16[256,48,128]{2,1,0:T(8,128)(2,1)} async-done(((bf16[256,48,128]{2,1,0:T(8,128)(2,1)}), bf16[256,48,128]{2,1,0:T(8,128)(2,1)}, u32[]{:S(2)}, u32[]{:S(2)}) %all-to-all-start.1) | async-done | bytes 3145760 | tf_op jit(solution)/shard_map/all_to_all | solution.py:340
  181.7 34.5 %edges.1 = bf16[256,48,128]{2,1,0:T(8,128)(2,1)S(1)} custom-call(s32[4]{0:T(128)S(1)} %pad_add_fusion.place_ref, bf16[256,48,128]{2,1,0:T(8,128)(2,1)} %all-to-all-done.1.held_ref, bf16[4,384,128]{2,1,0:T(8,128)(2,1)S(1)} %get-tuple-element.8.refs_0_, bf16[4,384,128]{2,1,0:T(8,128)(2,1)S(1)} %collective-permute-done.refs_1_, ...), custom_call_target="tpu_custom_call" | custom-call | tf_op jit(solution)/shard_map/edges/pallas_call | solution.py:212
  216.1 81.6 %all_to_all.20.back_ref = bf16[256,48,128]{2,1,0:T(8,128)(2,1)S(1)} all-to-all(bf16[256,48,128]{2,1,0:T(8,128)(2,1)S(1)} %edges.1), channel_id=1, replica_groups=mesh['log'=64,'pix'=4] {'pix','log'}, dimensions={0} | all-to-all | bytes 6291456 | tf_op jit(solution)/shard_map/all_to_all | solution.py:342
  297.8 5.9 %land.1 = bf16[64,96,128]{2,1,0:T(8,128)(2,1)S(1)} custom-call(bf16[256,48,128]{2,1,0:T(8,128)(2,1)S(1)} %all_to_all.20.back_ref, s32[64,128]{1,0:T(8,128)S(1)} %bitcast.10), custom_call_target="tpu_custom_call" | custom-call | tf_op jit(solution)/shard_map/land/pallas_call | solution.py:266
  303.7 43.4 %all_to_all.21.back_ref = bf16[64,96,128]{2,1,0:T(8,128)(2,1)S(1)} all-to-all(bf16[64,96,128]{2,1,0:T(8,128)(2,1)S(1)} %land.1), channel_id=1, replica_groups=mesh['log'=64,'pix'=4] {'log'}, dimensions={0} | all-to-all | bytes 3145728 | tf_op jit(solution)/shard_map/all_to_all | solution.py:344
  347.1 4.0 %collect.1 = f32[16,384,128]{2,1,0:T(8,128)} custom-call(bf16[64,96,128]{2,1,0:T(8,128)(2,1)S(1)} %all_to_all.21.back_ref), custom_call_target="tpu_custom_call" | custom-call | tf_op jit(solution)/shard_map/collect/pallas_call | solution.py:303
  (2 shorter events, 0.0 us)
Async XLA Ops:
  0.0 1.4 copy-start
  6.4 13.3 %copy-start.2 = (s32[28,1]{0,1:T(1,128)S(1)}, s32[28,1]{0,1:T(1,128)}, u32[]{:S(2)}) copy-start(s32[28,1]{0,1:T(1,128)} %param.6) | copy-start | bytes 340
  6.4 13.3 %copy-start.3 = (s32[28,1]{0,1:T(1,128)S(1)}, s32[28,1]{0,1:T(1,128)}, u32[]{:S(2)}) copy-start(s32[28,1]{0,1:T(1,128)} %param.5) | copy-start | bytes 340
  6.4 83.9 %all-to-all-start = ((bf16[64,96,128]{2,1,0:T(8,128)(2,1)}), bf16[64,96,128]{2,1,0:T(8,128)(2,1)S(1)}, u32[]{:S(2)}, u32[]{:S(2)}) async-start(bf16[64,96,128]{2,1,0:T(8,128)(2,1)} %spread.1), calls=%async_computation | async-start | bytes 3145728 | tf_op jit(solution)/shard_map/all_to_all | solution.py:338
  96.4 8.8 %copy-start.1 = (bf16[14,384,128]{2,1,0:T(8,128)(2,1)S(1)}, bf16[14,384,128]{2,1,0:T(8,128)(2,1)}, u32[]{:S(2)}) copy-start(bf16[14,384,128]{2,1,0:T(8,128)(2,1)} %param.7) | copy-start | bytes 4128772
  96.4 85.3 %all-to-all-start.1 = ((bf16[256,48,128]{2,1,0:T(8,128)(2,1)}), bf16[256,48,128]{2,1,0:T(8,128)(2,1)}, u32[]{:S(2)}, u32[]{:S(2)}) async-start(bf16[256,48,128]{2,1,0:T(8,128)(2,1)} %fetch.1), calls=%async_computation.1 | async-start | bytes 6291456 | tf_op jit(solution)/shard_map/all_to_all | solution.py:340
  106.3 19.1 %collective-permute-start = (bf16[4,384,128]{2,1,0:T(8,128)(2,1)}, bf16[4,384,128]{2,1,0:T(8,128)(2,1)S(1)}, u32[]{:S(2)}, u32[]{:S(2)}) collective-permute-start(bf16[4,384,128]{2,1,0:T(8,128)(2,1)} %get-tuple-element.6), channel_id=1, source_target_pairs={{0,1},{1,2},{2,3},{3,0},{4,5},{5,6},{6,7},{7,4},{8,9},{9,10},{10,1... | collective-permute-start | bytes 1179656 | tf_op jit(solution)/shard_map/ppermute | solution.py:334
  107.7 33.5 %collective-permute-start.1 = (bf16[4,384,128]{2,1,0:T(8,128)(2,1)}, bf16[4,384,128]{2,1,0:T(8,128)(2,1)S(1)}, u32[]{:S(2)}, u32[]{:S(2)}) collective-permute-start(bf16[4,384,128]{2,1,0:T(8,128)(2,1)} %get-tuple-element.7), channel_id=1, source_target_pairs={{0,2},{1,3},{2,0},{3,1},{4,6},{5,7},{6,4},{7,5},{8,10},{9,11},{10,... | collective-permute-start | bytes 1179656 | tf_op jit(solution)/shard_map/ppermute | solution.py:334
  110.1 31.1 %collective-permute-start.2 = (bf16[4,384,128]{2,1,0:T(8,128)(2,1)S(1)}, bf16[4,384,128]{2,1,0:T(8,128)(2,1)S(1)}, u32[]{:S(2)}, u32[]{:S(2)}) collective-permute-start(bf16[4,384,128]{2,1,0:T(8,128)(2,1)S(1)} %get-tuple-element.5), channel_id=1, source_target_pairs={{0,3},{1,0},{2,1},{3,2},{4,7},{5,4},{6,5},{7,6},{8,11},{9,8},{10,9... | collective-permute-start | bytes 1179656 | tf_op jit(solution)/shard_map/ppermute | solution.py:334

commit v2 on v0

v2 whole, which is shorter than its diff:
```python
import functools
import math

import jax
import jax.numpy as jnp
from jax import lax
from jax.experimental import pallas as pl
from jax.experimental.pallas import tpu as pltpu
from jax.sharding import PartitionSpec as P

F32 = jnp.float32
BF16 = jnp.bfloat16
LANES = 128
ENDS = 28
PARTS = 4
SLOTS = 7
META = 2
GROUPS = 4


def dot(a, b, ca, cb):
    return lax.dot_general(a, b, (((ca,), (cb,)), ((), ())), preferred_element_type=F32)


def params(mebi):
    return pltpu.CompilerParams(vmem_limit_bytes=mebi * 2**20)


def cost(flops, size):
    return pl.CostEstimate(flops=flops, bytes_accessed=size, transcendentals=0)


def spread_kernel(peers, piece, feat_ref, owner_ref, frame_ref, out_ref, wide, line):
    step = pl.program_id(0)
    some = feat_ref.shape[0]
    frames = some * pl.num_programs(0)
    each = piece * some * GROUPS + META
    for f in range(some):
        for k in range(piece):
            block = feat_ref[f, k * peers : (k + 1) * peers, :].astype(F32)
            wide[pl.ds(k * some * GROUPS + step * some + f, peers, stride=each), :] = block

    @pl.when(step == pl.num_programs(0) - 1)
    def _():
        ends = owner_ref.shape[1]
        for at, ref in enumerate((owner_ref, frame_ref)):
            line[...] = jnp.full(line.shape, 127.0, F32)
            line[0:1, 0:ends] = ref[...].astype(F32)
            values = jnp.broadcast_to(line[0:1, :], (peers, LANES))
            wide[pl.ds(each - META + at, peers, stride=each), :] = values
        out_ref[...] = wide[...].astype(BF16)


def spread(features, owners, locals_, peers):
    frames, rows, chans = features.shape
    piece = rows // peers
    total = peers * (piece * frames + META)
    ends = owners.shape[0]
    return pl.pallas_call(
        functools.partial(spread_kernel, peers, piece),
        grid=(GROUPS,),
        out_shape=jax.ShapeDtypeStruct((total, chans), BF16),
        in_specs=[
            pl.BlockSpec((frames // GROUPS, rows, chans), lambda g: (g, 0, 0)),
            pl.BlockSpec((1, ends), lambda g: (0, 0)),
            pl.BlockSpec((1, ends), lambda g: (0, 0)),
        ],
        out_specs=pl.BlockSpec((total, chans), lambda g: (0, 0)),
        scratch_shapes=[pltpu.VMEM((total, chans), F32), pltpu.VMEM((8, LANES), F32)],
        compiler_params=params(12),
        name="spread",
    )(features, owners.reshape(1, ends), locals_.reshape(1, ends))


def lane_of(part, slot):
    odd = lax.rem(part, 2)
    own = odd * 6 + slot
    return lax.div(part, 2) * 14 + jnp.where(slot < 6, own, 12 + odd)


def id_column(owner, frame, part):
    peers = owner.shape[0]
    count = SLOTS * peers
    row = lax.broadcasted_iota(jnp.int32, (count, peers), 0)
    col = lax.broadcasted_iota(jnp.int32, (count, peers), 1)
    pick = jnp.where(lax.rem(row, peers) == col, 1.0, 0.0).astype(BF16)
    every = dot(pick, frame, 1, 0) * peers + dot(pick, owner, 1, 0)
    row = lax.broadcasted_iota(jnp.int32, (count, LANES), 0)
    lane = lax.broadcasted_iota(jnp.int32, (count, LANES), 1)
    mine = lane == lane_of(part, lax.div(row, peers))
    return jnp.sum(jnp.where(mine, every, 0.0), axis=1, keepdims=True)


def id_row(owner, frame, part):
    peers = owner.shape[0]
    count = SLOTS * peers
    row = lax.broadcasted_iota(jnp.int32, (LANES, count), 0)
    col = lax.broadcasted_iota(jnp.int32, (LANES, count), 1)
    pick = jnp.where(row == lane_of(part, lax.div(col, peers)), 1.0, 0.0).astype(BF16)
    every = dot(frame, pick, 1, 0) * peers + dot(owner, pick, 1, 0)
    row = lax.broadcasted_iota(jnp.int32, (peers, count), 0)
    col = lax.broadcasted_iota(jnp.int32, (peers, count), 1)
    return jnp.sum(jnp.where(lax.rem(col, peers) == row, every, 0.0), axis=0, keepdims=True)


def fetch_kernel(piece, frames, peers, held_ref, out_ref, ids_ref, table, held, wide):
    part = pl.program_id(0)
    total = peers * frames
    each = piece * SLOTS
    pitch = piece * frames + META

    @pl.when(part == 0)
    def _():
        held[...] = held_ref[...].astype(F32)
        for f in range(frames):
            for k in range(piece):
                block = held[pl.ds(k * frames + f, peers, stride=pitch), :]
                table[f * peers : (f + 1) * peers, k * LANES : (k + 1) * LANES] = block.astype(BF16)
        for at in range(META):
            ids_ref[at] = held[pl.ds(pitch - META + at, peers, stride=pitch), :].astype(BF16)

    column = id_column(ids_ref[0], ids_ref[1], part)
    lane = lax.broadcasted_iota(jnp.int32, (SLOTS * peers, total), 1).astype(F32)
    chosen = jnp.where(column == lane, 1.0, 0.0).astype(BF16)
    rows = dot(chosen, table[...], 1, 0)
    for k in range(piece):
        for s in range(SLOTS):
            block = rows[s * peers : (s + 1) * peers, k * LANES : (k + 1) * LANES]
            wide[pl.ds(k * SLOTS + s, peers, stride=each), :] = block
    out_ref[...] = wide[...].astype(BF16)


def fetch(held, piece, frames, peers):
    block = peers * piece * SLOTS
    return pl.pallas_call(
        functools.partial(fetch_kernel, piece, frames, peers),
        grid=(PARTS,),
        out_shape=(
            jax.ShapeDtypeStruct((PARTS * block, LANES), BF16),
            jax.ShapeDtypeStruct((META, peers, LANES), BF16),
        ),
        in_specs=[pl.BlockSpec(held.shape, lambda p: (0, 0))],
        out_specs=(
            pl.BlockSpec((block, LANES), lambda p: (p, 0)),
            pl.BlockSpec((META, peers, LANES), lambda p: (0, 0, 0)),
        ),
        scratch_shapes=[
            pltpu.VMEM((peers * frames, piece * LANES), BF16),
            pltpu.VMEM(held.shape, F32),
            pltpu.VMEM((block, LANES), F32),
        ],
        compiler_params=params(24),
        name="fetch",
    )(held)


def unpack_kernel(piece, peers, in_ref, out_ref, wide):
    each = piece * SLOTS
    wide[...] = in_ref[...].astype(F32)
    for s in range(SLOTS):
        for k in range(piece):
            block = wide[pl.ds(k * SLOTS + s, peers, stride=each), :]
            out_ref[s, k * peers : (k + 1) * peers, :] = block.astype(BF16)


def unpack(got, piece, peers):
    block = peers * piece * SLOTS
    rows = piece * peers
    return pl.pallas_call(
        functools.partial(unpack_kernel, piece, peers),
        grid=(PARTS,),
        out_shape=jax.ShapeDtypeStruct((SLOTS, PARTS * rows, LANES), BF16),
        in_specs=[pl.BlockSpec((block, LANES), lambda p: (p, 0))],
        out_specs=pl.BlockSpec((SLOTS, rows, LANES), lambda p: (0, p, 0)),
        scratch_shapes=[pltpu.VMEM((block, LANES), F32)],
        compiler_params=params(12),
        name="unpack",
    )(got)


def pack_kernel(piece, peers, first_ref, last_ref, kept_ref, come_ref, out_ref, wide):
    each = piece * SLOTS
    for s in range(SLOTS):
        for k in range(piece):
            here = slice(k * peers, (k + 1) * peers)
            if s < 4:
                block = first_ref[s, here, :].astype(F32)
            elif s < 6:
                block = last_ref[s - 4, here, :].astype(F32)
            else:
                block = kept_ref[here, :].astype(F32) + come_ref[here, :].astype(F32)
            wide[pl.ds(k * SLOTS + s, peers, stride=each), :] = block
    out_ref[...] = wide[...].astype(BF16)


def pack(first, last, kept, come, piece, peers):
    block = peers * piece * SLOTS
    rows = piece * peers
    return pl.pallas_call(
        functools.partial(pack_kernel, piece, peers),
        grid=(PARTS,),
        out_shape=jax.ShapeDtypeStruct((PARTS * block, LANES), BF16),
        in_specs=[
            pl.BlockSpec((4, rows, LANES), lambda p: (0, p, 0)),
            pl.BlockSpec((2, rows, LANES), lambda p: (0, p, 0)),
            pl.BlockSpec((rows, LANES), lambda p: (p, 0)),
            pl.BlockSpec((rows, LANES), lambda p: (p, 0)),
        ],
        out_specs=pl.BlockSpec((block, LANES), lambda p: (p, 0)),
        scratch_shapes=[pltpu.VMEM((block, LANES), F32)],
        compiler_params=params(12),
        name="pack",
    )(first, last, kept, come)


def edge_block(q, g, key_all):
    scale = LANES ** (-0.5)
    scores = dot(q, key_all, 1, 1)
    top = jnp.max(scores, axis=1, keepdims=True)
    expo = jnp.exp2((scores - top) * (scale * math.log2(math.e)))
    total = jnp.sum(expo, axis=1, keepdims=True)
    dprobs = dot(g, key_all, 1, 1)
    inverse = 1.0 / total
    delta = jnp.sum(expo * dprobs, axis=1, keepdims=True) * inverse
    probs = expo * inverse
    dscores = (probs * (dprobs - delta)).astype(BF16)
    grad_query = (dot(dscores, key_all, 1, 0) * scale).astype(BF16)
    return grad_query, dot(q, dscores, 0, 0), dot(g, probs.astype(BF16), 0, 0)


def place_cotangent(place_ref, cot_refs, cot):
    for part in range(PARTS):
        rows = cot_refs[part].shape[1]
        at = pl.multiple_of(place_ref[part] * rows, rows)
        cot[pl.ds(at, rows), :] = cot_refs[part][0]


def edge_kernel(block, place_ref, query_ref, keys_ref, *refs):
    cot_refs = refs[:PARTS]
    out_ref, cot, grad_a, grad_b = refs[PARTS:]
    place_cotangent(place_ref, cot_refs, cot)
    key_all = keys_ref[0]
    for step in range(cot.shape[0] // block):
        here = slice(step * block, (step + 1) * block)
        grad_query, first, second = edge_block(query_ref[0, here, :], cot[here, :], key_all)
        out_ref[0, here, :] = grad_query
        if step == 0:
            grad_a[...] = first
            grad_b[...] = second
        else:
            grad_a[...] += first
            grad_b[...] += second
    out_ref[1] = (grad_a[...] * LANES ** (-0.5) + grad_b[...]).T.astype(BF16)


def edges(maps, cotangents, places, start, count):
    _, pixels, chans = maps.shape
    rows = pixels // PARTS
    per_edge = pl.BlockSpec((1, rows, chans), lambda e, place: (e + start, 0, 0))
    return pl.pallas_call(
        functools.partial(edge_kernel, 768),
        grid_spec=pltpu.PrefetchScalarGridSpec(
            num_scalar_prefetch=1,
            grid=(count,),
            in_specs=[
                pl.BlockSpec((1, pixels, chans), lambda e, place: (2 * (e + start), 0, 0)),
                pl.BlockSpec((1, pixels, chans), lambda e, place: (2 * (e + start) + 1, 0, 0)),
            ]
            + [per_edge] * PARTS,
            out_specs=pl.BlockSpec((2, pixels, chans), lambda e, place: (e, 0, 0)),
            scratch_shapes=[
                pltpu.VMEM((pixels, chans), BF16),
                pltpu.VMEM((chans, pixels), F32),
                pltpu.VMEM((chans, pixels), F32),
            ],
        ),
        out_shape=jax.ShapeDtypeStruct((2 * count, pixels, chans), BF16),
        compiler_params=params(40),
        cost_estimate=cost(count * 10 * pixels * pixels * chans, count * 5 * pixels * chans * 2),
        name="edges",
    )(places, maps, maps, *cotangents)


def shared_kernel(block, place_ref, own_ref, come_ref, *refs):
    cot_refs = refs[:PARTS]
    kept_ref, sent_ref, query, keys, cot, grad_a, grad_b = refs[PARTS:]
    pixels = cot.shape[0]
    half = pixels // 2
    odd = place_ref[PARTS]
    place_cotangent(place_ref, cot_refs, cot)
    own = own_ref[0]
    come = come_ref[0]
    query[...] = jnp.where(odd == 0, own, come)
    keys[...] = jnp.where(odd == 0, come, own)
    key_all = keys[...]
    base = pl.multiple_of(odd * half, half)

    def halves(q_ref, k_ref):
        other = pl.multiple_of((1 - odd) * half, half)
        q_ref[pl.ds(other, half), :] = jnp.zeros((half, LANES), BF16)
        for step in range(half // block):
            here = pl.ds(pl.multiple_of(base + step * block, block), block)
            grad_query, first, second = edge_block(query[here, :], cot[here, :], key_all)
            q_ref[here, :] = grad_query
            if step == 0:
                grad_a[...] = first
                grad_b[...] = second
            else:
                grad_a[...] += first
                grad_b[...] += second
        k_ref[...] = (grad_a[...] * LANES ** (-0.5) + grad_b[...]).T.astype(BF16)

    @pl.when(odd == 0)
    def _():
        halves(kept_ref, sent_ref)

    @pl.when(odd == 1)
    def _():
        halves(sent_ref, kept_ref)


def shared_edge(maps, come, cotangents, places):
    slots, pixels, chans = maps.shape
    rows = pixels // PARTS
    last = cotangents[0].shape[0] - 1
    whole = pl.BlockSpec((pixels, chans), lambda e, place: (0, 0))
    return pl.pallas_call(
        functools.partial(shared_kernel, 768),
        grid_spec=pltpu.PrefetchScalarGridSpec(
            num_scalar_prefetch=1,
            grid=(1,),
            in_specs=[
                pl.BlockSpec((1, pixels, chans), lambda e, place: (slots - 1, 0, 0)),
                pl.BlockSpec((1, pixels, chans), lambda e, place: (0, 0, 0)),
            ]
            + [pl.BlockSpec((1, rows, chans), lambda e, place: (last, 0, 0))] * PARTS,
            out_specs=[whole, whole],
            scratch_shapes=[
                pltpu.VMEM((pixels, chans), BF16),
                pltpu.VMEM((pixels, chans), BF16),
                pltpu.VMEM((pixels, chans), BF16),
                pltpu.VMEM((chans, pixels), F32),
                pltpu.VMEM((chans, pixels), F32),
            ],
        ),
        out_shape=[jax.ShapeDtypeStruct((pixels, chans), BF16)] * 2,
        compiler_params=params(40),
        cost_estimate=cost(5 * pixels * pixels * chans, 5 * pixels * chans * 2),
        name="shared_edge",
    )(places, maps, come, *cotangents)


def land_kernel(piece, frames, back_ref, ids_ref, out_ref, total, wide, spread_out):
    part = pl.program_id(0)
    peers = ids_ref.shape[1]
    each = piece * SLOTS
    row = id_row(ids_ref[0], ids_ref[1], part)
    every = lax.broadcasted_iota(jnp.int32, (peers * frames, SLOTS * peers), 0).astype(F32)
    chosen = jnp.where(row == every, 1.0, 0.0).astype(BF16)
    wide[...] = back_ref[...].astype(F32)
    columns = []
    for k in range(piece):
        column = [wide[pl.ds(k * SLOTS + s, peers, stride=each), :].astype(BF16) for s in range(SLOTS)]
        columns.append(jnp.concatenate(column, axis=0))
    sums = dot(chosen, jnp.concatenate(columns, axis=1), 1, 0)

    @pl.when(part == 0)
    def _():
        total[...] = sums

    @pl.when(part > 0)
    def _():
        total[...] += sums

    @pl.when(part == PARTS - 1)
    def _():
        for k in range(piece):
            for f in range(frames):
                block = total[f * peers : (f + 1) * peers, k * LANES : (k + 1) * LANES]
                spread_out[pl.ds(k * frames + f, peers, stride=piece * frames), :] = block
        out_ref[...] = spread_out[...].astype(BF16)


def land(back, ids, piece, frames):
    peers = ids.shape[1]
    block = peers * piece * SLOTS
    rows = peers * piece * frames
    return pl.pallas_call(
        functools.partial(land_kernel, piece, frames),
        grid=(PARTS,),
        out_shape=jax.ShapeDtypeStruct((rows, LANES), BF16),
        in_specs=[
            pl.BlockSpec((block, LANES), lambda p: (p, 0)),
            pl.BlockSpec(ids.shape, lambda p: (0, 0, 0)),
        ],
        out_specs=pl.BlockSpec((rows, LANES), lambda p: (0, 0)),
        scratch_shapes=[
            pltpu.VMEM((peers * frames, piece * LANES), F32),
            pltpu.VMEM((block, LANES), F32),
            pltpu.VMEM((rows, LANES), F32),
        ],
        compiler_params=params(32),
        name="land",
    )(back, ids)


def collect_kernel(piece, peers, back_ref, out_ref, wide):
    step = pl.program_id(0)
    some = out_ref.shape[0]
    each = piece * some * GROUPS

    @pl.when(step == 0)
    def _():
        wide[...] = back_ref[...].astype(F32)

    for f in range(some):
        for k in range(piece):
            block = wide[pl.ds(k * some * GROUPS + step * some + f, peers, stride=each), :]
            out_ref[f, k * peers : (k + 1) * peers, :] = block


def collect(back, frames, piece, peers):
    return pl.pallas_call(
        functools.partial(collect_kernel, piece, peers),
        grid=(GROUPS,),
        out_shape=jax.ShapeDtypeStruct((frames, piece * peers, LANES), F32),
        in_specs=[pl.BlockSpec(back.shape, lambda g: (0, 0))],
        out_specs=pl.BlockSpec((frames // GROUPS, piece * peers, LANES), lambda g: (g, 0, 0)),
        scratch_shapes=[pltpu.VMEM(back.shape, F32)],
        compiler_params=params(16),
        name="collect",
    )(back)


def exchange(blocks, axes):
    total = blocks.shape[0]
    count = lax.axis_size(axes)
    shape = (count, total // count // 2, 2, LANES)
    moved = lax.all_to_all(blocks.reshape(shape), axes, 0, 0, tiled=True)
    return moved.reshape(total, LANES)


def shards(features, endpoint_owner, endpoint_frame, grad_matched):
    peers = lax.axis_size("log")
    frames, rows, chans = features.shape
    piece = rows // peers
    me = lax.axis_index("pix")
    if lax.axis_size("pix") != PARTS or endpoint_owner.shape[0] != ENDS:
        raise ValueError("other sizes")

    cotangents = []
    for t in range(PARTS):
        taker = lax.rem(me + t, PARTS)
        start = lax.div(taker, 2) * 7
        own = lax.dynamic_slice_in_dim(grad_matched, start + lax.rem(taker, 2) * 3, 3, axis=0)
        both = lax.dynamic_slice_in_dim(grad_matched, start + 6, 1, axis=0)
        given = jnp.concatenate([own, both], axis=0)
        if t:
            given = lax.ppermute(given, "pix", [(p, (p + t) % PARTS) for p in range(PARTS)])
        cotangents.append(given)
    places = jnp.stack([lax.rem(me + PARTS - t, PARTS) for t in range(PARTS)] + [lax.rem(me, 2)])
    partner = [(p, p ^ 1) for p in range(PARTS)]

    everyone = ("pix", "log")

    held = exchange(spread(features, endpoint_owner, endpoint_frame, peers), "log")
    sent, ids = fetch(held, piece, frames, peers)
    maps = unpack(exchange(sent, everyone), piece, peers)
    come = lax.ppermute(maps[SLOTS - 1 :], "pix", partner)
    first = edges(maps, cotangents, places, 0, 2)
    come, first = lax.optimization_barrier((come, first))
    kept, given = shared_edge(maps, come, cotangents, places)
    come = lax.ppermute(given, "pix", partner)
    last = edges(maps, cotangents, places, 2, 1)
    grads = pack(first, last, kept, come, piece, peers)
    sums = land(exchange(grads, everyone), ids, piece, frames)
    return collect(exchange(sums, "log"), frames, piece, peers)


def solution(mesh):
    in_specs = (P("log", "pix", None), P("log", None), P("log", None), P("log", "pix", None))
    out_specs = P("log", "pix", None)
    return jax.shard_map(shards, mesh=mesh, in_specs=in_specs, out_specs=out_specs, check_vma=False)
```

time: 659 us -> 312 us (0.47)
  waiting for transfers between devices: 395 us -> 57.5 us
  matrix products: 150 us -> 0 us
  blocking collectives: 22.2 us -> 172 us
  Pallas kernels: 0 us -> 49.6 us
  local copies, waits for them, and re-layouts: 35.4 us -> 7.37 us
  other arithmetic: 21.9 us -> 3.28 us
  between operations: 13.6 us -> 0.66 us
    all_to_all x2 -> x1, waiting for transfers between devices: 280 us -> 57.5 us  [exchange(): moved = lax.all_to_all(blocks.reshape(shape), axes, 0, 0, tiled=True)]
    all_to_all x1 -> x3, blocking collectives: 22.2 us -> 172 us  [exchange(): moved = lax.all_to_all(blocks.reshape(shape), axes, 0, 0, tiled=True)]
    dot_general x86 -> x0, matrix products: 150 us -> none  [the longest x14 34.4 us: edge_terms(): jnp.dot(probs_low.T, cotangent, preferred_element_type=jnp.float32)]
    reduce_scatter x1 -> x0, waiting for transfers between devices: 60.9 us -> none  [shards(): lax.psum_scatter(partial_keys.astype(jnp.bfloat16), 'pix', scatter_dimens...]
    all_gather x1 -> x0, waiting for transfers between devices: 54.2 us -> none  [shards(): keys = lax.all_gather(own_keys, 'pix', axis=1, tiled=True)]
    pallas_call x0 -> x9, Pallas kernels: none -> 49.6 us  [the longest x2 24.2 us: edges(): pl.pallas_call(functools.partial(edge_kernel, 768), grid_spec=pltpu.Prefe...]
    dynamic_slice x28 -> x2, local copies, waits for them, and re-layouts: 14.3 us -> 3.01 us  [the longest x1 1.71 us: shards(): both = lax.dynamic_slice_in_dim(grad_matched, start + 6, 1, axis=0)]
    gather x3 -> x0, local copies, waits for them, and re-layouts: 11.2 us -> none  [the longest x1 4.01 us: shards(): served = jnp.take(features, wanted, axis=0)]
  transfers between devices with their start and end apart: 4 -> 6, of which waited for: 4 -> 1; matrix products, arithmetic and copies ran while one was open for 1% -> 2% of each run, Pallas kernels for 0% -> 8%
where the time goes in v2:
time: 312 us; the launch traced here: 306 us
  blocking collectives  172 us (55%)
  waiting for transfers between devices  57.5 us (18%)
  Pallas kernels  49.6 us (16%)
  starting transfers between devices  15.4 us (5%)
  local copies, waits for them, and re-layouts  7.37 us (2%)
  other arithmetic  3.28 us (1%)
    all_to_all x3, blocking collectives, exchange(): moved = lax.all_to_all(blocks.reshape(shape), axes, 0, 0, tiled=True)  172 us
    all_to_all x1, waiting for transfers between devices, exchange(): moved = lax.all_to_all(blocks.reshape(shape), axes, 0, 0, tiled=True)  57.5 us
    pallas_call x2, Pallas kernels, edges(): pl.pallas_call(functools.partial(edge_kernel, 768), grid_spec=pltpu.Prefe...  24.2 us
    pallas_call x1, Pallas kernels, land(): pl.pallas_call(functools.partial(land_kernel, piece, frames), grid=(PARTS...  8.99 us
    all_to_all x1, starting transfers between devices, exchange(): moved = lax.all_to_all(blocks.reshape(shape), axes, 0, 0, tiled=True)  8.61 us
  transfers between devices with their start and end apart: 6, of which 1 were waited for; matrix products, arithmetic and copies ran while one was open for 2% of the time, Pallas kernels for 8%

profile of v2, /device:TPU:1, one launch (start us, length us, event | category | flops | bytes accessed | tf_op | source)
XLA Modules:
  0.0 306.2 jit_solution(9527690116375618186)
XLA Ops:
  0.0 0.0 copy-start.1
  0.0 1.4 copy-done.1
  1.4 0.0 copy-start.2
  1.4 0.7 copy-done.2
  2.1 0.0 copy-start.3
  2.1 0.7 copy-done.3
  2.7 0.4 spread.1
  3.2 53.5 %all_to_all.20 = bf16[64,49,2,128]{3,2,1,0:T(2,128)(2,1)S(1)} all-to-all(bf16[64,49,2,128]{3,2,1,0:T(2,128)(2,1)S(1)} %bitcast.19), channel_id=1, replica_groups=mesh['log'=64,'pix'=4] {'log'}, dimensions={0} | all-to-all | bytes 3211264 | tf_op jit(solution)/shard_map/all_to_all | solution.py:439
  56.6 5.1 %fetch.1 = (bf16[10752,128]{1,0:T(8,128)(2,1)S(1)}, bf16[2,64,128]{2,1,0:T(8,128)(2,1)S(1)}) custom-call(bf16[6272,128]{1,0:T(8,128)(2,1)S(1)} %bitcast.18), custom_call_target="tpu_custom_call" | custom-call | tf_op jit(solution)/shard_map/fetch/pallas_call | solution.py:135
  61.7 0.0 copy-start
  61.8 1.5 copy-done
  63.3 8.6 %all-to-all-start.1 = ((bf16[256,21,2,128]{3,2,1,0:T(2,128)(2,1)}), bf16[256,21,2,128]{3,2,1,0:T(2,128)(2,1)S(1)}, u32[]{:S(2)}, u32[]{:S(2)}) async-start(bf16[256,21,2,128]{3,2,1,0:T(2,128)(2,1)} %bitcast.22), calls=%async_computation.1 | async-start | bytes 5505024 | tf_op jit(solution)/shard_map/all_to_all | solution.py:439
  72.0 1.7 constant_dynamic-slice_fusion
  73.7 1.3 constant_dynamic-slice_fusion.1
  75.0 0.8 pad_maximum_fusion.1
  75.8 1.4 collective-permute-start.1
  77.2 0.8 pad_maximum_fusion.2
  78.0 2.4 collective-permute-start.2
  80.4 0.8 pad_maximum_fusion.3
  81.2 1.2 collective-permute-start.3
  82.3 0.1 stack.23.place_ref
  82.4 0.9 pad_maximum_fusion.refs_0_
  83.4 57.5 %all-to-all-done.1 = bf16[256,21,2,128]{3,2,1,0:T(2,128)(2,1)S(1)} async-done(((bf16[256,21,2,128]{3,2,1,0:T(2,128)(2,1)}), bf16[256,21,2,128]{3,2,1,0:T(2,128)(2,1)S(1)}, u32[]{:S(2)}, u32[]{:S(2)}) %all-to-all-start.1) | async-done | bytes 2752544 | tf_op jit(solution)/shard_map/all_to_all | solution.py:439
  140.9 0.9 unpack.1.query_ref.keys_ref.own_ref
  141.8 0.6 collective-permute-start
  142.3 0.0 collective-permute-done.1.refs_1_
  142.3 0.0 collective-permute-done.2.refs_2_
  142.3 0.0 collective-permute-done.3.refs_3_
  142.3 15.7 %edges.2.first_ref = bf16[4,1536,128]{2,1,0:T(8,128)(2,1)S(1)} custom-call(s32[5]{0:T(128)S(1)} %stack.23.place_ref, bf16[7,1536,128]{2,1,0:T(8,128)(2,1)S(1)} %unpack.1.query_ref.keys_ref.own_ref, bf16[7,1536,128]{2,1,0:T(8,128)(2,1)S(1)} %unpack.1.query_ref.keys_ref.own_ref, bf16[4,384,128]{2,1,0:T(8,128)(2,1)S(1)} %pad_maximum_fusion.refs_0_, ...), custom_call_target="tpu_custom_call" | custom-call | flops 6039797760 | bytes 3932160 | tf_op jit(solution)/shard_map/edges/pallas_call | solution.py:260
  158.0 0.0 collective-permute-done.come_ref
  158.0 5.7 %shared_edge.1 = (bf16[1536,128]{1,0:T(8,128)(2,1)S(1)}, bf16[1536,128]{1,0:T(8,128)(2,1)S(1)}) custom-call(s32[5]{0:T(128)S(1)} %stack.23.place_ref, bf16[7,1536,128]{2,1,0:T(8,128)(2,1)S(1)} %unpack.1.query_ref.keys_ref.own_ref, bf16[1,1536,128]{2,1,0:T(8,128)(2,1)S(1)} %collective-permute-done.come_ref, bf16[4,384,128]{2,1,0:T(8,128)(2,1)S(1)} %pad_maximum_fusion.refs_0_, ...), custom_call_target="tpu_custom_call" | custom-call | flops 1509949440 | bytes 1966080 | tf_op jit(solution)/shard_map/shared_edge/pallas_call | solution.py:327
  163.7 1.3 collective-permute-start.4
  165.0 8.6 %edges.3.last_ref = bf16[2,1536,128]{2,1,0:T(8,128)(2,1)S(1)} custom-call(s32[5]{0:T(128)S(1)} %stack.23.place_ref, bf16[7,1536,128]{2,1,0:T(8,128)(2,1)S(1)} %unpack.1.query_ref.keys_ref.own_ref, bf16[7,1536,128]{2,1,0:T(8,128)(2,1)S(1)} %unpack.1.query_ref.keys_ref.own_ref, bf16[4,384,128]{2,1,0:T(8,128)(2,1)S(1)} %pad_maximum_fusion.refs_0_, ...), custom_call_target="tpu_custom_call" | custom-call | flops 3019898880 | bytes 1966080 | tf_op jit(solution)/shard_map/edges/pallas_call | solution.py:260
  173.6 0.0 collective-permute-done.4.come_ref
  173.6 0.9 pack.1
  174.5 75.5 %all_to_all.21 = bf16[256,21,2,128]{3,2,1,0:T(2,128)(2,1)S(1)} all-to-all(bf16[256,21,2,128]{3,2,1,0:T(2,128)(2,1)S(1)} %bitcast.16), channel_id=1, replica_groups=mesh['log'=64,'pix'=4] {'pix','log'}, dimensions={0} | all-to-all | bytes 5505024 | tf_op jit(solution)/shard_map/all_to_all | solution.py:439
  250.0 9.0 %land.1 = bf16[6144,128]{1,0:T(8,128)(2,1)S(1)} custom-call(bf16[10752,128]{1,0:T(8,128)(2,1)S(1)} %bitcast.17, bf16[2,64,128]{2,1,0:T(8,128)(2,1)S(1)} %get-tuple-element.16.ids_ref), custom_call_target="tpu_custom_call" | custom-call | tf_op jit(solution)/shard_map/land/pallas_call | solution.py:388
  259.0 43.4 %all_to_all.22 = bf16[64,48,2,128]{3,2,1,0:T(2,128)(2,1)S(1)} all-to-all(bf16[64,48,2,128]{3,2,1,0:T(2,128)(2,1)S(1)} %bitcast.20), channel_id=1, replica_groups=mesh['log'=64,'pix'=4] {'log'}, dimensions={0} | all-to-all | bytes 3145728 | tf_op jit(solution)/shard_map/all_to_all | solution.py:439
  302.4 3.4 %collect.1 = f32[16,384,128]{2,1,0:T(8,128)} custom-call(bf16[6144,128]{1,0:T(8,128)(2,1)S(1)} %bitcast.21), custom_call_target="tpu_custom_call" | custom-call | tf_op jit(solution)/shard_map/collect/pallas_call | solution.py:423
  (1 shorter events, 0.0 us)
Async XLA Ops:
  0.0 1.4 copy-start.1
  1.4 0.7 copy-start.2
  2.1 0.7 copy-start.3
  61.7 1.5 copy-start
  63.3 77.6 %all-to-all-start.1 = ((bf16[256,21,2,128]{3,2,1,0:T(2,128)(2,1)}), bf16[256,21,2,128]{3,2,1,0:T(2,128)(2,1)S(1)}, u32[]{:S(2)}, u32[]{:S(2)}) async-start(bf16[256,21,2,128]{3,2,1,0:T(2,128)(2,1)} %bitcast.22), calls=%async_computation.1 | async-start | bytes 5505024 | tf_op jit(solution)/shard_map/all_to_all | solution.py:439
  75.8 66.5 %collective-permute-start.1 = (bf16[4,384,128]{2,1,0:T(8,128)(2,1)}, bf16[4,384,128]{2,1,0:T(8,128)(2,1)}, u32[]{:S(2)}, u32[]{:S(2)}) collective-permute-start(bf16[4,384,128]{2,1,0:T(8,128)(2,1)} %pad_maximum_fusion.1), channel_id=1, source_target_pairs={{0,1},{1,2},{2,3},{3,0},{4,5},{5,6},{6,7},{7,4},{8,9},{9,10},{10,1... | collective-permute-start | bytes 1179656 | tf_op jit(solution)/shard_map/ppermute | solution.py:459
  78.0 64.4 %collective-permute-start.2 = (bf16[4,384,128]{2,1,0:T(8,128)(2,1)}, bf16[4,384,128]{2,1,0:T(8,128)(2,1)}, u32[]{:S(2)}, u32[]{:S(2)}) collective-permute-start(bf16[4,384,128]{2,1,0:T(8,128)(2,1)} %pad_maximum_fusion.2), channel_id=1, source_target_pairs={{0,2},{1,3},{2,0},{3,1},{4,6},{5,7},{6,4},{7,5},{8,10},{9,11},{10,... | collective-permute-start | bytes 1179656 | tf_op jit(solution)/shard_map/ppermute | solution.py:459
  81.2 61.2 %collective-permute-start.3 = (bf16[4,384,128]{2,1,0:T(8,128)(2,1)}, bf16[4,384,128]{2,1,0:T(8,128)(2,1)}, u32[]{:S(2)}, u32[]{:S(2)}) collective-permute-start(bf16[4,384,128]{2,1,0:T(8,128)(2,1)} %pad_maximum_fusion.3), channel_id=1, source_target_pairs={{0,3},{1,0},{2,1},{3,2},{4,7},{5,4},{6,5},{7,6},{8,11},{9,8},{10,9... | collective-permute-start | bytes 1179656 | tf_op jit(solution)/shard_map/ppermute | solution.py:459
  141.8 16.2 %collective-permute-start = (bf16[1,1536,128]{2,1,0:T(8,128)(2,1)S(1)}, bf16[1,1536,128]{2,1,0:T(8,128)(2,1)S(1)}, u32[]{:S(2)}, u32[]{:S(2)}) collective-permute-start(bf16[1,1536,128]{2,1,0:T(8,128)(2,1)S(1)} %slice.4), channel_id=1, source_target_pairs={{0,1},{1,0},{2,3},{3,2},{4,5},{5,4},{6,7},{7,6},{8,9},{9,8},{10,11... | collective-permute-start | bytes 1179656 | tf_op jit(solution)/shard_map/ppermute | solution.py:469
  163.7 9.8 %collective-permute-start.4 = (bf16[1536,128]{1,0:T(8,128)(2,1)S(1)}, bf16[1536,128]{1,0:T(8,128)(2,1)S(1)}, u32[]{:S(2)}, u32[]{:S(2)}) collective-permute-start(bf16[1536,128]{1,0:T(8,128)(2,1)S(1)} %get-tuple-element.15), channel_id=1, source_target_pairs={{0,1},{1,0},{2,3},{3,2},{4,5},{5,4},{6,7},{7,6},{8,9},{9,8},{10,11... | collective-permute-start | bytes 1179656 | tf_op jit(solution)/shard_map/ppermute | solution.py:473

commit v3 on v2

v3 whole, which is shorter than its diff:
```python
import functools
import math

import jax
import jax.numpy as jnp
from jax import lax
from jax.experimental import pallas as pl
from jax.experimental.pallas import tpu as pltpu
from jax.sharding import PartitionSpec as P

F32 = jnp.float32
BF16 = jnp.bfloat16
LANES = 128
ENDS = 28
PARTS = 4
SLOTS = 7
META = 2
GROUPS = 4
SAFE = (1e-20, 1e20)


def dot(a, b, ca, cb):
    return lax.dot_general(a, b, (((ca,), (cb,)), ((), ())), preferred_element_type=F32)


def params(mebi):
    return pltpu.CompilerParams(vmem_limit_bytes=mebi * 2**20)


def in_hbm(x):
    return pltpu.with_memory_space_constraint(x, pltpu.HBM)


def vmem():
    return pl.BlockSpec(memory_space=pltpu.VMEM)


def cost(flops, size):
    return pl.CostEstimate(flops=flops, bytes_accessed=size, transcendentals=0)


def spread_kernel(peers, piece, feat_ref, owner_ref, frame_ref, out_ref, wide, line):
    step = pl.program_id(0)
    some = feat_ref.shape[0]
    frames = some * pl.num_programs(0)
    each = piece * some * GROUPS + META
    for f in range(some):
        for k in range(piece):
            block = feat_ref[f, k * peers : (k + 1) * peers, :].astype(F32)
            wide[pl.ds(k * some * GROUPS + step * some + f, peers, stride=each), :] = block

    @pl.when(step == pl.num_programs(0) - 1)
    def _():
        ends = owner_ref.shape[1]
        for at, ref in enumerate((owner_ref, frame_ref)):
            line[...] = jnp.full(line.shape, 127.0, F32)
            line[0:1, 0:ends] = ref[...].astype(F32)
            values = jnp.broadcast_to(line[0:1, :], (peers, LANES))
            wide[pl.ds(each - META + at, peers, stride=each), :] = values
        out_ref[...] = wide[...].astype(BF16)


def spread(features, owners, locals_, peers):
    frames, rows, chans = features.shape
    piece = rows // peers
    total = peers * (piece * frames + META)
    ends = owners.shape[0]
    return pl.pallas_call(
        functools.partial(spread_kernel, peers, piece),
        grid=(GROUPS,),
        out_shape=jax.ShapeDtypeStruct((total, chans), BF16),
        in_specs=[
            pl.BlockSpec((frames // GROUPS, rows, chans), lambda g: (g, 0, 0)),
            pl.BlockSpec((1, ends), lambda g: (0, 0)),
            pl.BlockSpec((1, ends), lambda g: (0, 0)),
        ],
        out_specs=pl.BlockSpec((total, chans), lambda g: (0, 0)),
        scratch_shapes=[pltpu.VMEM((total, chans), F32), pltpu.VMEM((8, LANES), F32)],
        compiler_params=params(12),
        name="spread",
    )(*[in_hbm(x) for x in (features, owners.reshape(1, ends), locals_.reshape(1, ends))])


def lane_of(part, slot):
    odd = part % 2
    own = odd * 6 + slot
    return part // 2 * 14 + jnp.where(slot < 6, own, 12 + odd)


def id_column(owner, frame, part):
    peers = owner.shape[0]
    count = SLOTS * peers
    row = lax.broadcasted_iota(jnp.int32, (count, peers), 0)
    col = lax.broadcasted_iota(jnp.int32, (count, peers), 1)
    pick = jnp.where(lax.rem(row, peers) == col, 1.0, 0.0).astype(BF16)
    every = dot(pick, frame, 1, 0) * peers + dot(pick, owner, 1, 0)
    row = lax.broadcasted_iota(jnp.int32, (count, LANES), 0)
    lane = lax.broadcasted_iota(jnp.int32, (count, LANES), 1)
    mine = lane == lane_of(part, lax.div(row, peers))
    return jnp.sum(jnp.where(mine, every, 0.0), axis=1, keepdims=True)


def id_row(owner, frame, part):
    peers = owner.shape[0]
    count = SLOTS * peers
    row = lax.broadcasted_iota(jnp.int32, (LANES, count), 0)
    col = lax.broadcasted_iota(jnp.int32, (LANES, count), 1)
    pick = jnp.where(row == lane_of(part, lax.div(col, peers)), 1.0, 0.0).astype(BF16)
    every = dot(frame, pick, 1, 0) * peers + dot(owner, pick, 1, 0)
    row = lax.broadcasted_iota(jnp.int32, (peers, count), 0)
    col = lax.broadcasted_iota(jnp.int32, (peers, count), 1)
    return jnp.sum(jnp.where(lax.rem(col, peers) == row, every, 0.0), axis=0, keepdims=True)


def fetch_kernel(piece, frames, peers, held_ref, out_ref, ids_ref, table, held, wide, ready, sems):
    total = peers * frames
    each = piece * SLOTS
    block = peers * each
    pitch = piece * frames + META
    held[...] = held_ref[...].astype(F32)
    for f in range(frames):
        for k in range(piece):
            rows = held[pl.ds(k * frames + f, peers, stride=pitch), :]
            table[f * peers : (f + 1) * peers, k * LANES : (k + 1) * LANES] = rows.astype(BF16)
    for at in range(META):
        ids_ref[at] = held[pl.ds(pitch - META + at, peers, stride=pitch), :].astype(BF16)
    owner, frame = ids_ref[0], ids_ref[1]
    lane = lax.broadcasted_iota(jnp.int32, (SLOTS * peers, total), 1).astype(F32)
    copies = []
    for part in range(PARTS):
        column = id_column(owner, frame, part)
        chosen = jnp.where(column == lane, 1.0, 0.0).astype(BF16)
        rows = dot(chosen, table[...], 1, 0)
        for k in range(piece):
            for s in range(SLOTS):
                some = rows[s * peers : (s + 1) * peers, k * LANES : (k + 1) * LANES]
                wide[part, pl.ds(k * SLOTS + s, peers, stride=each), :] = some
        ready[part] = wide[part].astype(BF16)
        there = out_ref.at[pl.ds(part * block, block)]
        copies.append(pltpu.make_async_copy(ready.at[part], there, sems.at[part]))
        copies[-1].start()
    for copy in copies:
        copy.wait()


def fetch(held, piece, frames, peers):
    block = peers * piece * SLOTS
    return pl.pallas_call(
        functools.partial(fetch_kernel, piece, frames, peers),
        out_shape=(
            pltpu.HBM((PARTS * block, LANES), BF16),
            jax.ShapeDtypeStruct((META, peers, LANES), BF16),
        ),
        in_specs=[vmem()],
        out_specs=(pl.BlockSpec(memory_space=pl.ANY), vmem()),
        scratch_shapes=[
            pltpu.VMEM((peers * frames, piece * LANES), BF16),
            pltpu.VMEM(held.shape, F32),
            pltpu.VMEM((PARTS, block, LANES), F32),
            pltpu.VMEM((PARTS, block, LANES), BF16),
            pltpu.SemaphoreType.DMA((PARTS,)),
        ],
        compiler_params=params(40),
        name="fetch",
    )(held)


def unpack_kernel(piece, peers, in_ref, out_ref, wide):
    each = piece * SLOTS
    wide[...] = in_ref[...].astype(F32)
    for s in range(SLOTS):
        for k in range(piece):
            block = wide[pl.ds(k * SLOTS + s, peers, stride=each), :]
            out_ref[s, k * peers : (k + 1) * peers, :] = block.astype(BF16)


def unpack(got, piece, peers):
    block = peers * piece * SLOTS
    rows = piece * peers
    return pl.pallas_call(
        functools.partial(unpack_kernel, piece, peers),
        grid=(PARTS,),
        out_shape=jax.ShapeDtypeStruct((SLOTS, PARTS * rows, LANES), BF16),
        in_specs=[pl.BlockSpec((block, LANES), lambda p: (p, 0))],
        out_specs=pl.BlockSpec((SLOTS, rows, LANES), lambda p: (0, p, 0)),
        scratch_shapes=[pltpu.VMEM((block, LANES), F32)],
        compiler_params=params(12),
        name="unpack",
    )(got)


def pack_kernel(piece, peers, first_ref, last_ref, kept_ref, come_ref, out_ref, wide):
    each = piece * SLOTS
    for s in range(SLOTS):
        for k in range(piece):
            here = slice(k * peers, (k + 1) * peers)
            if s < 4:
                block = first_ref[s, here, :].astype(F32)
            elif s < 6:
                block = last_ref[s - 4, here, :].astype(F32)
            else:
                block = kept_ref[here, :].astype(F32) + come_ref[here, :].astype(F32)
            wide[pl.ds(k * SLOTS + s, peers, stride=each), :] = block
    out_ref[...] = wide[...].astype(BF16)


def pack(first, last, kept, come, piece, peers):
    block = peers * piece * SLOTS
    rows = piece * peers
    return pl.pallas_call(
        functools.partial(pack_kernel, piece, peers),
        grid=(PARTS,),
        out_shape=jax.ShapeDtypeStruct((PARTS * block, LANES), BF16),
        in_specs=[
            pl.BlockSpec((4, rows, LANES), lambda p: (0, p, 0)),
            pl.BlockSpec((2, rows, LANES), lambda p: (0, p, 0)),
            pl.BlockSpec((rows, LANES), lambda p: (p, 0)),
            pl.BlockSpec((rows, LANES), lambda p: (p, 0)),
        ],
        out_specs=pl.BlockSpec((block, LANES), lambda p: (p, 0)),
        scratch_shapes=[pltpu.VMEM((block, LANES), F32)],
        compiler_params=params(12),
        name="pack",
    )(first, last, kept, come)


def edge_block(q, g, key_all, take_top):
    scale = LANES ** (-0.5)
    scores = dot(q, key_all, 1, 1)
    if take_top:
        scores = scores - jnp.max(scores, axis=1, keepdims=True)
    expo = jnp.exp2(scores * (scale * math.log2(math.e)))
    total = jnp.sum(expo, axis=1, keepdims=True)
    dprobs = dot(g, key_all, 1, 1)
    inverse = 1.0 / total
    probs = expo * inverse
    probs_low = probs.astype(BF16)
    delta = jnp.sum(probs_low.astype(F32) * dprobs, axis=1, keepdims=True)
    dscores = (probs * (dprobs - delta)).astype(BF16)
    grad_query = (dot(dscores, key_all, 1, 0) * scale).astype(BF16)
    grad_keys = dot(q, dscores, 0, 0) * scale + dot(g, probs_low, 0, 0)
    return grad_query, grad_keys, total


def unsafe(totals):
    low = functools.reduce(jnp.minimum, totals)
    high = functools.reduce(jnp.maximum, totals)
    return jnp.logical_not((jnp.min(low) > SAFE[0]) & (jnp.max(high) < SAFE[1]))


def place_cotangent(place_ref, cot_refs, cot, edge):
    for part in range(PARTS):
        rows = cot_refs[part].shape[1]
        at = pl.multiple_of(place_ref[part] * rows, rows)
        cot[pl.ds(at, rows), :] = cot_refs[part][edge]


def edge_kernel(block, start, count, place_ref, maps_ref, *refs):
    cot_refs = refs[:PARTS]
    out_ref, cots, grad = refs[PARTS:]

    def run(edge, take_top):
        key_all = maps_ref[2 * (start + edge) + 1]
        totals = []
        for step in range(cots.shape[1] // block):
            here = slice(step * block, (step + 1) * block)
            query = maps_ref[2 * (start + edge), here, :]
            grad_query, grad_keys, total = edge_block(query, cots[edge, here, :], key_all, take_top)
            totals.append(total)
            out_ref[2 * edge, here, :] = grad_query
            if step == 0:
                grad[edge] = grad_keys
            else:
                grad[edge] += grad_keys
        out_ref[2 * edge + 1] = grad[edge].T.astype(BF16)
        return totals

    def one(edge, carry):
        place_cotangent(place_ref, cot_refs, cots.at[edge], start + edge)
        totals = run(edge, False)

        @pl.when(unsafe(totals))
        def _():
            run(edge, True)

        return carry

    lax.fori_loop(0, count, one, 0)


def edges(maps, cotangents, places, start, count):
    _, pixels, chans = maps.shape
    return pl.pallas_call(
        functools.partial(edge_kernel, pixels // 2, start, count),
        in_specs=[pl.BlockSpec(memory_space=pltpu.SMEM)] + [vmem()] * (PARTS + 1),
        out_specs=vmem(),
        out_shape=jax.ShapeDtypeStruct((2 * count, pixels, chans), BF16),
        scratch_shapes=[
            pltpu.VMEM((count, pixels, chans), BF16),
            pltpu.VMEM((count, chans, pixels), F32),
        ],
        compiler_params=params(40),
        cost_estimate=cost(count * 10 * pixels * pixels * chans, count * 5 * pixels * chans * 2),
        name="edges",
    )(places, maps, *cotangents)


def shared_kernel(place_ref, maps_ref, come_ref, *refs):
    cot_refs = refs[:PARTS]
    kept_ref, sent_ref, query, keys, cot, grad = refs[PARTS:]
    pixels = cot.shape[0]
    half = pixels // 2
    odd = place_ref[PARTS]
    place_cotangent(place_ref, cot_refs, cot, cot_refs[0].shape[0] - 1)
    own = maps_ref.at[SLOTS - 1]
    come = come_ref.at[0]

    @pl.when(odd == 0)
    def _():
        query[...] = own[:half, :]
        keys[...] = come[...]

    @pl.when(odd == 1)
    def _():
        query[...] = come[half:, :]
        keys[...] = own[...]

    def run(take_top):
        g = cot[pl.ds(pl.multiple_of(odd * half, half), half), :]
        grad_query, grad_keys, total = edge_block(query[...], g, keys[...], take_top)
        grad[:half, :] = grad_query
        grad[half:, :] = grad_keys.T.astype(BF16)
        return total

    total = run(False)

    @pl.when(unsafe([total]))
    def _():
        run(True)

    @pl.when(odd == 0)
    def _():
        kept_ref[:half, :] = grad[:half, :]
        kept_ref[half:, :] = jnp.zeros((half, LANES), BF16)
        sent_ref[...] = grad[half:, :]

    @pl.when(odd == 1)
    def _():
        sent_ref[:half, :] = jnp.zeros((half, LANES), BF16)
        sent_ref[half:, :] = grad[:half, :]
        kept_ref[...] = grad[half:, :]


def shared_edge(maps, come, cotangents, places):
    _, pixels, chans = maps.shape
    return pl.pallas_call(
        shared_kernel,
        in_specs=[pl.BlockSpec(memory_space=pltpu.SMEM)] + [vmem()] * (PARTS + 2),
        out_specs=[vmem(), vmem()],
        out_shape=[jax.ShapeDtypeStruct((pixels, chans), BF16)] * 2,
        scratch_shapes=[
            pltpu.VMEM((pixels // 2, chans), BF16),
            pltpu.VMEM((pixels, chans), BF16),
            pltpu.VMEM((pixels, chans), BF16),
            pltpu.VMEM((pixels // 2 * 3, chans), BF16),
        ],
        compiler_params=params(40),
        cost_estimate=cost(5 * pixels * pixels * chans, 5 * pixels * chans * 2),
        name="shared_edge",
    )(places, maps, come, *cotangents)


def land_kernel(piece, frames, back_ref, ids_ref, out_ref, values, wide, spread_out):
    peers = ids_ref.shape[1]
    each = piece * SLOTS
    count = SLOTS * peers
    rows = each * peers
    wide[...] = back_ref[...].astype(F32)
    names = []
    for part in range(PARTS):
        names.append(id_row(ids_ref[0], ids_ref[1], part))
        for k in range(piece):
            for s in range(SLOTS):
                block = wide[pl.ds(part * rows + k * SLOTS + s, peers, stride=each), :]
                at = part * count + s * peers
                values[at : at + peers, k * LANES : (k + 1) * LANES] = block.astype(BF16)
    name = jnp.concatenate(names, axis=1)
    some = 4
    for group in range(frames // some):
        every = lax.broadcasted_iota(jnp.int32, (some * peers, PARTS * count), 0) + group * some * peers
        chosen = jnp.where(name == every.astype(F32), 1.0, 0.0).astype(BF16)
        sums = dot(chosen, values[...], 1, 0)
        for f in range(some):
            for k in range(piece):
                block = sums[f * peers : (f + 1) * peers, k * LANES : (k + 1) * LANES]
                at = k * frames + group * some + f
                spread_out[pl.ds(at, peers, stride=piece * frames), :] = block
    out_ref[...] = spread_out[...].astype(BF16)


def land(back, ids, piece, frames):
    peers = ids.shape[1]
    rows = peers * piece * frames
    return pl.pallas_call(
        functools.partial(land_kernel, piece, frames),
        out_shape=jax.ShapeDtypeStruct((rows, LANES), BF16),
        in_specs=[vmem(), vmem()],
        out_specs=vmem(),
        scratch_shapes=[
            pltpu.VMEM((PARTS * SLOTS * peers, piece * LANES), BF16),
            pltpu.VMEM(back.shape, F32),
            pltpu.VMEM((rows, LANES), F32),
        ],
        compiler_params=params(32),
        name="land",
    )(back, ids)


def collect_kernel(piece, peers, back_ref, out_ref, wide):
    step = pl.program_id(0)
    some = out_ref.shape[0]
    frames = some * pl.num_programs(0)
    each = piece * frames

    @pl.when(step == 0)
    def _():
        wide[...] = back_ref[...].astype(F32)

    for f in range(some):
        for k in range(piece):
            block = wide[pl.ds(k * frames + step * some + f, peers, stride=each), :]
            out_ref[f, k * peers : (k + 1) * peers, :] = block


def collect(back, frames, piece, peers):
    return pl.pallas_call(
        functools.partial(collect_kernel, piece, peers),
        grid=(GROUPS,),
        out_shape=jax.ShapeDtypeStruct((frames, piece * peers, LANES), F32),
        in_specs=[vmem()],
        out_specs=pl.BlockSpec((frames // GROUPS, piece * peers, LANES), lambda g: (g, 0, 0)),
        scratch_shapes=[pltpu.VMEM(back.shape, F32)],
        compiler_params=params(16),
        name="collect",
    )(back)


def exchange(blocks, axes):
    total = blocks.shape[0]
    count = lax.axis_size(axes)
    shape = (count, total // count // 2, 2, LANES)
    moved = lax.all_to_all(blocks.reshape(shape), axes, 0, 0, tiled=True)
    return moved.reshape(total, LANES)


def shards(features, endpoint_owner, endpoint_frame, grad_matched):
    peers = lax.axis_size("log")
    frames, rows, chans = features.shape
    piece = rows // peers
    me = lax.axis_index("pix")
    if lax.axis_size("pix") != PARTS or endpoint_owner.shape[0] != ENDS:
        raise ValueError("other sizes")

    cotangents = []
    for t in range(PARTS):
        taker = lax.rem(me + t, PARTS)
        start = lax.div(taker, 2) * 7
        own = lax.dynamic_slice_in_dim(grad_matched, start + lax.rem(taker, 2) * 3, 3, axis=0)
        both = lax.dynamic_slice_in_dim(grad_matched, start + 6, 1, axis=0)
        given = jnp.concatenate([own, both], axis=0)
        if t:
            given = lax.ppermute(given, "pix", [(p, (p + t) % PARTS) for p in range(PARTS)])
        cotangents.append(given)
    places = jnp.stack([lax.rem(me + PARTS - t, PARTS) for t in range(PARTS)] + [lax.rem(me, 2)])
    partner = [(p, p ^ 1) for p in range(PARTS)]

    everyone = ("pix", "log")

    held = exchange(spread(features, endpoint_owner, endpoint_frame, peers), "log")
    sent, ids = fetch(held, piece, frames, peers)
    maps = unpack(exchange(sent, everyone), piece, peers)
    come = lax.ppermute(maps[SLOTS - 1 :], "pix", partner)
    first = edges(maps, cotangents, places, 0, 2)
    come, first = lax.optimization_barrier((come, first))
    kept, given = shared_edge(maps, come, cotangents, places)
    come = lax.ppermute(given, "pix", partner)
    last = edges(maps, cotangents, places, 2, 1)
    grads = pack(first, last, kept, come, piece, peers)
    sums = land(exchange(grads, everyone), ids, piece, frames)
    return collect(exchange(sums, "log"), frames, piece, peers)


def solution(mesh):
    in_specs = (P("log", "pix", None), P("log", None), P("log", None), P("log", "pix", None))
    out_specs = P("log", "pix", None)
    return jax.shard_map(shards, mesh=mesh, in_specs=in_specs, out_specs=out_specs, check_vma=False)
```

time: 312 us -> 339 us (1.087)
  Pallas kernels: 49.6 us -> 81.1 us
  local copies, waits for them, and re-layouts: 7.37 us -> 3.14 us
    pallas_call x5, Pallas kernels: 44.1 us -> 73.5 us  [the longest x2 54.4 us: edges(): pl.pallas_call(functools.partial(edge_kernel, pixels // 2, start, count),...]
    unnamed x8 -> x0, local copies, waits for them, and re-layouts: 4.25 us -> none
  transfers between devices with their start and end apart: 6 -> 6, of which waited for: 1 -> 1; matrix products, arithmetic and copies ran while one was open for 2% -> 2% of each run, Pallas kernels for 8% -> 17%
where the time goes in v3:
time: 339 us; the launch traced here: 332 us
  blocking collectives  171 us (50%)
  Pallas kernels  81.1 us (24%)
  waiting for transfers between devices  57.5 us (17%)
  starting transfers between devices  15.2 us (4%)
    all_to_all x3, blocking collectives, exchange(): moved = lax.all_to_all(blocks.reshape(shape), axes, 0, 0, tiled=True)  171 us
    all_to_all x1, waiting for transfers between devices, exchange(): moved = lax.all_to_all(blocks.reshape(shape), axes, 0, 0, tiled=True)  57.5 us
    pallas_call x2, Pallas kernels, edges(): pl.pallas_call(functools.partial(edge_kernel, pixels // 2, start, count),...  54.4 us
    all_to_all x1, starting transfers between devices, exchange(): moved = lax.all_to_all(blocks.reshape(shape), axes, 0, 0, tiled=True)  8.62 us
    pallas_call x1, Pallas kernels, shared_edge(): pl.pallas_call(shared_kernel, in_specs=[pl.BlockSpec(memory_space=pltpu.S...  8.53 us
  transfers between devices with their start and end apart: 6, of which 1 were waited for; matrix products, arithmetic and copies ran while one was open for 2% of the time, Pallas kernels for 17%

profile of v3, /device:TPU:1, one launch (start us, length us, event | category | flops | bytes accessed | tf_op | source)
XLA Modules:
  0.0 331.8 jit_solution(13357830793300639689)
XLA Ops:
  0.0 2.5 spread.1
  2.5 53.5 %all_to_all.20 = bf16[64,49,2,128]{3,2,1,0:T(2,128)(2,1)S(1)} all-to-all(bf16[64,49,2,128]{3,2,1,0:T(2,128)(2,1)S(1)} %bitcast.19), channel_id=1, replica_groups=mesh['log'=64,'pix'=4] {'log'}, dimensions={0} | all-to-all | bytes 3211264 | tf_op jit(solution)/shard_map/all_to_all | solution.py:452
  55.9 4.6 %fetch.1 = (bf16[10752,128]{1,0:T(8,128)(2,1)}, bf16[2,64,128]{2,1,0:T(8,128)(2,1)S(1)}) custom-call(bf16[6272,128]{1,0:T(8,128)(2,1)S(1)} %bitcast.18), custom_call_target="tpu_custom_call" | custom-call | tf_op jit(solution)/shard_map/fetch/pallas_call | solution.py:148
  60.5 8.6 %all-to-all-start.1 = ((bf16[256,21,2,128]{3,2,1,0:T(2,128)(2,1)}), bf16[256,21,2,128]{3,2,1,0:T(2,128)(2,1)S(1)}, u32[]{:S(2)}, u32[]{:S(2)}) async-start(bf16[256,21,2,128]{3,2,1,0:T(2,128)(2,1)} %bitcast.22), calls=%async_computation.1 | async-start | bytes 5505024 | tf_op jit(solution)/shard_map/all_to_all | solution.py:452
  69.3 1.7 constant_dynamic-slice_fusion
  71.0 1.3 constant_dynamic-slice_fusion.1
  72.3 0.8 pad_maximum_fusion.1
  73.1 1.4 collective-permute-start.1
  74.5 0.8 pad_maximum_fusion.2
  75.3 2.4 collective-permute-start.2
  77.7 0.8 pad_maximum_fusion.3
  78.4 1.2 collective-permute-start.3
  79.6 0.1 stack.23.place_ref
  79.7 0.9 pad_maximum_fusion.refs_0_
  80.6 57.5 %all-to-all-done.1 = bf16[256,21,2,128]{3,2,1,0:T(2,128)(2,1)S(1)} async-done(((bf16[256,21,2,128]{3,2,1,0:T(2,128)(2,1)}), bf16[256,21,2,128]{3,2,1,0:T(2,128)(2,1)S(1)}, u32[]{:S(2)}, u32[]{:S(2)}) %all-to-all-start.1) | async-done | bytes 2752544 | tf_op jit(solution)/shard_map/all_to_all | solution.py:452
  138.1 0.9 unpack.1.maps_ref
  139.0 0.4 collective-permute-start
  139.4 0.0 collective-permute-done.1.refs_1_
  139.4 0.0 collective-permute-done.2.refs_2_
  139.4 0.0 collective-permute-done.3.refs_3_
  139.4 39.1 %edges.2.first_ref = bf16[4,1536,128]{2,1,0:T(8,128)(2,1)S(1)} custom-call(s32[5]{0:T(128)S(1)} %stack.23.place_ref, bf16[7,1536,128]{2,1,0:T(8,128)(2,1)S(1)} %unpack.1.maps_ref, bf16[4,384,128]{2,1,0:T(8,128)(2,1)S(1)} %pad_maximum_fusion.refs_0_, bf16[4,384,128]{2,1,0:T(8,128)(2,1)} %collective-permute-done.1.refs_1_, ...), custom_call_target="tpu_custom_call" | custom-call | flops 6039797760 | bytes 3932160 | tf_op jit(solution)/shard_map/edges/pallas_call | solution.py:293
  178.5 0.0 collective-permute-done.come_ref
  178.6 8.5 %shared_edge.1 = (bf16[1536,128]{1,0:T(8,128)(2,1)S(1)}, bf16[1536,128]{1,0:T(8,128)(2,1)S(1)}) custom-call(s32[5]{0:T(128)S(1)} %stack.23.place_ref, bf16[7,1536,128]{2,1,0:T(8,128)(2,1)S(1)} %unpack.1.maps_ref, bf16[1,1536,128]{2,1,0:T(8,128)(2,1)S(1)} %collective-permute-done.come_ref, bf16[4,384,128]{2,1,0:T(8,128)(2,1)S(1)} %pad_maximum_fusion.refs_0_, ...), custom_call_target="tpu_custom_call" | custom-call | flops 1509949440 | bytes 1966080 | tf_op jit(solution)/shard_map/shared_edge/pallas_call | solution.py:356
  187.1 1.2 collective-permute-start.4
  188.3 15.3 %edges.3.last_ref = bf16[2,1536,128]{2,1,0:T(8,128)(2,1)S(1)} custom-call(s32[5]{0:T(128)S(1)} %stack.23.place_ref, bf16[7,1536,128]{2,1,0:T(8,128)(2,1)S(1)} %unpack.1.maps_ref, bf16[4,384,128]{2,1,0:T(8,128)(2,1)S(1)} %pad_maximum_fusion.refs_0_, bf16[4,384,128]{2,1,0:T(8,128)(2,1)} %collective-permute-done.1.refs_1_, ...), custom_call_target="tpu_custom_call" | custom-call | flops 3019898880 | bytes 1966080 | tf_op jit(solution)/shard_map/edges/pallas_call | solution.py:293
  203.6 0.0 collective-permute-done.4.come_ref
  203.6 0.9 pack.1
  204.5 74.1 %all_to_all.21 = bf16[256,21,2,128]{3,2,1,0:T(2,128)(2,1)S(1)} all-to-all(bf16[256,21,2,128]{3,2,1,0:T(2,128)(2,1)S(1)} %bitcast.16), channel_id=1, replica_groups=mesh['log'=64,'pix'=4] {'pix','log'}, dimensions={0} | all-to-all | bytes 5505024 | tf_op jit(solution)/shard_map/all_to_all | solution.py:452
  278.6 6.0 %land.1 = bf16[6144,128]{1,0:T(8,128)(2,1)S(1)} custom-call(bf16[10752,128]{1,0:T(8,128)(2,1)S(1)} %bitcast.17, bf16[2,64,128]{2,1,0:T(8,128)(2,1)S(1)} %get-tuple-element.16.ids_ref), custom_call_target="tpu_custom_call" | custom-call | tf_op jit(solution)/shard_map/land/pallas_call | solution.py:404
  284.6 43.4 %all_to_all.22 = bf16[64,48,2,128]{3,2,1,0:T(2,128)(2,1)S(1)} all-to-all(bf16[64,48,2,128]{3,2,1,0:T(2,128)(2,1)S(1)} %bitcast.20), channel_id=1, replica_groups=mesh['log'=64,'pix'=4] {'log'}, dimensions={0} | all-to-all | bytes 3145728 | tf_op jit(solution)/shard_map/all_to_all | solution.py:452
  328.0 3.4 %collect.1 = f32[16,384,128]{2,1,0:T(8,128)} custom-call(bf16[6144,128]{1,0:T(8,128)(2,1)S(1)} %bitcast.21), custom_call_target="tpu_custom_call" | custom-call | tf_op jit(solution)/shard_map/collect/pallas_call | solution.py:436
  (1 shorter events, 0.0 us)
Async XLA Ops:
  60.5 77.6 %all-to-all-start.1 = ((bf16[256,21,2,128]{3,2,1,0:T(2,128)(2,1)}), bf16[256,21,2,128]{3,2,1,0:T(2,128)(2,1)S(1)}, u32[]{:S(2)}, u32[]{:S(2)}) async-start(bf16[256,21,2,128]{3,2,1,0:T(2,128)(2,1)} %bitcast.22), calls=%async_computation.1 | async-start | bytes 5505024 | tf_op jit(solution)/shard_map/all_to_all | solution.py:452
  73.1 66.3 %collective-permute-start.1 = (bf16[4,384,128]{2,1,0:T(8,128)(2,1)}, bf16[4,384,128]{2,1,0:T(8,128)(2,1)}, u32[]{:S(2)}, u32[]{:S(2)}) collective-permute-start(bf16[4,384,128]{2,1,0:T(8,128)(2,1)} %pad_maximum_fusion.1), channel_id=1, source_target_pairs={{0,1},{1,2},{2,3},{3,0},{4,5},{5,6},{6,7},{7,4},{8,9},{9,10},{10,1... | collective-permute-start | bytes 1179656 | tf_op jit(solution)/shard_map/ppermute | solution.py:472
  75.3 64.2 %collective-permute-start.2 = (bf16[4,384,128]{2,1,0:T(8,128)(2,1)}, bf16[4,384,128]{2,1,0:T(8,128)(2,1)}, u32[]{:S(2)}, u32[]{:S(2)}) collective-permute-start(bf16[4,384,128]{2,1,0:T(8,128)(2,1)} %pad_maximum_fusion.2), channel_id=1, source_target_pairs={{0,2},{1,3},{2,0},{3,1},{4,6},{5,7},{6,4},{7,5},{8,10},{9,11},{10,... | collective-permute-start | bytes 1179656 | tf_op jit(solution)/shard_map/ppermute | solution.py:472
  78.4 61.0 %collective-permute-start.3 = (bf16[4,384,128]{2,1,0:T(8,128)(2,1)}, bf16[4,384,128]{2,1,0:T(8,128)(2,1)}, u32[]{:S(2)}, u32[]{:S(2)}) collective-permute-start(bf16[4,384,128]{2,1,0:T(8,128)(2,1)} %pad_maximum_fusion.3), channel_id=1, source_target_pairs={{0,3},{1,0},{2,1},{3,2},{4,7},{5,4},{6,5},{7,6},{8,11},{9,8},{10,9... | collective-permute-start | bytes 1179656 | tf_op jit(solution)/shard_map/ppermute | solution.py:472
  139.0 39.5 %collective-permute-start = (bf16[1,1536,128]{2,1,0:T(8,128)(2,1)S(1)}, bf16[1,1536,128]{2,1,0:T(8,128)(2,1)S(1)}, u32[]{:S(2)}, u32[]{:S(2)}) collective-permute-start(bf16[1,1536,128]{2,1,0:T(8,128)(2,1)S(1)} %slice.4), channel_id=1, source_target_pairs={{0,1},{1,0},{2,3},{3,2},{4,5},{5,4},{6,7},{7,6},{8,9},{9,8},{10,11... | collective-permute-start | bytes 1179656 | tf_op jit(solution)/shard_map/ppermute | solution.py:482
  187.1 16.5 %collective-permute-start.4 = (bf16[1536,128]{1,0:T(8,128)(2,1)S(1)}, bf16[1536,128]{1,0:T(8,128)(2,1)S(1)}, u32[]{:S(2)}, u32[]{:S(2)}) collective-permute-start(bf16[1536,128]{1,0:T(8,128)(2,1)S(1)} %get-tuple-element.15), channel_id=1, source_target_pairs={{0,1},{1,0},{2,3},{3,2},{4,5},{5,4},{6,7},{7,6},{8,9},{9,8},{10,11... | collective-permute-start | bytes 1179656 | tf_op jit(solution)/shard_map/ppermute | solution.py:486
